TPU v7x, 32 devices: a whole 2x2x4 slice. The times are simulated.
32 devices in a mesh: dp: 8 (over y, x, core), seq: 4 (over z).
Axes of the slice: x: 2, y: 2, z: 4, core: 2. Of those that a mesh axis runs over, the one named last changes fastest.
Arguments:
- tokens: bfloat16 [16, 1024, 768], P('dp', 'seq'), may hold values from -6 to 6
- seg_starts: int32 [16, 8], P('dp'), may hold values from 0 to 1023, as said below
- w_qkv: bfloat16 [768, 2304], replicated, may hold values from -0.21875 to 0.21875
- b_query: float32 [768], replicated, may hold values from -3 to 3
- b_value: float32 [768], replicated, may hold values from -3 to 3
- w_out: bfloat16 [768, 768], replicated, may hold values from -0.875 to 0.875
- b_out: float32 [768], replicated, may hold values from -3 to 3
- gain_one: float32 [768], replicated, may hold values from 0.5 to 1.5
- beta_one: float32 [768], replicated, may hold values from -3 to 3
- w_up: bfloat16 [768, 3072], replicated, may hold values from -0.21875 to 0.21875
- b_up: float32 [3072], replicated, may hold values from -3 to 3
- w_down: bfloat16 [3072, 768], replicated, may hold values from -0.109375 to 0.109375
- b_down: float32 [768], replicated, may hold values from -3 to 3
- gain_two: float32 [768], replicated, may hold values from 0.5 to 1.5
- beta_two: float32 [768], replicated, may hold values from -3 to 3
- cotangent: bfloat16 [16, 1024, 768], P('dp', 'seq'), may hold values from -6 to 6
Outputs:
- mixed: bfloat16 [16, 1024, 768], P('dp', 'seq')
- cls_rows: bfloat16 [16, 8, 768], P('dp', None, 'seq')
- grad_tokens: bfloat16 [16, 1024, 768], P('dp', 'seq')
- grad_w_qkv: float32 [768, 2304], replicated
- grad_b_query: float32 [768], replicated
- grad_b_value: float32 [768], replicated
- grad_w_out: float32 [768, 768], replicated
- grad_b_out: float32 [768], replicated
- grad_gain_one: float32 [768], replicated
- grad_beta_one: float32 [768], replicated
- grad_w_up: float32 [768, 3072], replicated
- grad_b_up: float32 [3072], replicated
- grad_w_down: float32 [3072, 768], replicated
- grad_b_down: float32 [768], replicated
- grad_gain_two: float32 [768], replicated
- grad_beta_two: float32 [768], replicated
Inputs may be any that keep to these rules, and one draw needn't show every extreme that they name: `seg_starts`: in each row the starts rise strictly from 0; one segment of the row, never the last, which one drawn, begins before position 128 and reaches past 7 * 128; every other segment has at most 16 positions.
All inputs are finite; a program needn't handle non-finite values.
Results may differ from a plain program's by a relative error of at most 0.024.
Values may be sent and summed in bfloat16 or wider, within the bound.
No kernel may reach another device: no remote copies, remote signals or barrier semaphores. Data moves between devices by JAX's collectives and lax.ppermute only.
A program may use at most 192 MiB of HBM per device.

v0:
```python
from functools import partial

import jax
import jax.numpy as jnp
from jax import lax
from jax.sharding import PartitionSpec as P

HEADS = 12


negative = -1e30


def seg_index(starts, positions):
    return jnp.sum((starts[:, :, None] <= positions[None, None, :]).astype(jnp.int32), axis=1)


def norm_rows(h, gain, beta):
    mean = jnp.mean(h, axis=-1, keepdims=True)
    cent = h - mean
    var = jnp.mean(cent * cent, axis=-1, keepdims=True)
    return cent * lax.rsqrt(var + 1e-06) * gain + beta


def outer_sum(left, right):
    left_flat = left.reshape(-1, left.shape[-1])
    right_flat = right.reshape(-1, right.shape[-1])
    return lax.dot_general(
        left_flat, right_flat, (((0,), (0,)), ((), ())), preferred_element_type=jnp.float32
    )


def column_sum(values):
    return jnp.sum(values.astype(jnp.float32), axis=(0, 1))


def spread_heads(values, head):
    return jnp.repeat(jnp.swapaxes(values, 1, 2), head, axis=2)


def masked_scores(query4, key_piece, query_seg, key_seg, head, scale):
    rows, count, width = key_piece.shape
    key4 = key_piece.reshape(rows, count, width // head, head)
    scores = jnp.einsum("rqhd,rkhd->rhqk", query4, key4, preferred_element_type=jnp.float32) * scale
    mask = query_seg[:, None, :, None] == key_seg[:, None, None, :]
    return (jnp.where(mask, scores, negative), mask)


def on_device(
    tokens,
    seg_starts,
    w_qkv,
    b_query,
    b_value,
    w_out,
    b_out,
    gain_one,
    beta_one,
    w_up,
    b_up,
    w_down,
    b_down,
    gain_two,
    beta_two,
    cotangent,
):
    rows, group, width = tokens.shape
    head = width // HEADS
    scale = 1.0 / float(head) ** 0.5
    seq_count = lax.axis_size("seq")
    offset = lax.axis_index("seq") * group
    positions = offset + jnp.arange(group, dtype=jnp.int32)
    query_seg = seg_index(seg_starts, positions)
    qkv = jnp.dot(tokens, w_qkv, preferred_element_type=jnp.float32)
    query_b = (qkv[..., :width] + b_query).astype(jnp.bfloat16)
    key_b = qkv[..., width : 2 * width].astype(jnp.bfloat16)
    value_b = (qkv[..., 2 * width :] + b_value).astype(jnp.bfloat16)
    query4 = query_b.reshape(rows, group, HEADS, head)
    add_key_piece = lax.all_gather(key_b, "seq", axis=1, tiled=True)
    add_value_piece = lax.all_gather(value_b, "seq", axis=1, tiled=True)
    add_count = add_key_piece.shape[1]
    add_key_seg = seg_index(seg_starts, jnp.arange(add_count, dtype=jnp.int32))
    add_scores, add_mask = masked_scores(query4, add_key_piece, query_seg, add_key_seg, head, scale)
    high = jnp.full((rows, HEADS, group), negative, jnp.float32)
    accum = jnp.zeros((rows, group, width), jnp.float32)
    new_high = jnp.maximum(high, jnp.max(add_scores, axis=-1))
    weights = jnp.where(add_mask, jnp.exp(add_scores - new_high[..., None]), 0.0)
    fade = jnp.exp(high - new_high)
    total = jnp.sum(weights, axis=-1)
    add_value4 = add_value_piece.reshape(rows, add_count, HEADS, head)
    mixed_part = jnp.einsum(
        "rhqk,rkhd->rqhd",
        weights.astype(jnp.bfloat16),
        add_value4,
        preferred_element_type=jnp.float32,
    )
    accum = accum * spread_heads(fade, head) + mixed_part.reshape(rows, group, width)
    high, total, accum = (new_high, total, accum)
    attn = accum / spread_heads(total, head)
    lse = high + jnp.log(total)
    attn_b = attn.astype(jnp.bfloat16)
    tokens_f = tokens.astype(jnp.float32)
    branch = jnp.dot(attn_b, w_out, preferred_element_type=jnp.float32) + b_out
    h1 = tokens_f + branch
    n1 = norm_rows(h1, gain_one, beta_one)
    n1_b = n1.astype(jnp.bfloat16)
    pre = jnp.dot(n1_b, w_up, preferred_element_type=jnp.float32) + b_up
    gelu_exact = partial(jax.nn.gelu, approximate=False)
    act, gelu_pull = jax.vjp(gelu_exact, pre)
    act_b = act.astype(jnp.bfloat16)
    ffn = jnp.dot(act_b, w_down, preferred_element_type=jnp.float32) + b_down
    h2 = n1 + ffn
    out, norm_two_pull = jax.vjp(norm_rows, h2, gain_two, beta_two)
    mixed = out.astype(jnp.bfloat16)
    pick = (seg_starts[:, :, None] == positions[None, None, :]).astype(jnp.bfloat16)
    cls_part = jnp.einsum("rjc,rcd->rjd", pick, mixed, preferred_element_type=jnp.float32)
    cls_rows = lax.psum_scatter(
        cls_part.astype(jnp.bfloat16), "seq", scatter_dimension=2, tiled=True
    )
    dh2, grad_gain_two, grad_beta_two = norm_two_pull(cotangent.astype(jnp.float32))
    dffn = dh2.astype(jnp.bfloat16)
    grad_w_down = outer_sum(act_b, dffn)
    grad_b_down = column_sum(dffn)
    dact = jnp.dot(dffn, w_down.T, preferred_element_type=jnp.float32)
    dpre = gelu_pull(dact)[0].astype(jnp.bfloat16)
    grad_w_up = outer_sum(n1_b, dpre)
    grad_b_up = column_sum(dpre)
    dn1 = dh2 + jnp.dot(dpre, w_up.T, preferred_element_type=jnp.float32)
    norm_one_pull = jax.vjp(norm_rows, h1, gain_one, beta_one)[1]
    dh1, grad_gain_one, grad_beta_one = norm_one_pull(dn1)
    dbranch = dh1.astype(jnp.bfloat16)
    grad_w_out = outer_sum(attn_b, dbranch)
    grad_b_out = column_sum(dbranch)
    dattn_b = jnp.dot(dbranch, w_out.T, preferred_element_type=jnp.float32).astype(jnp.bfloat16)
    dattn4 = dattn_b.reshape(rows, group, HEADS, head)
    delta = jnp.swapaxes(
        jnp.sum((dattn_b.astype(jnp.float32) * attn).reshape(rows, group, HEADS, head), axis=-1),
        1,
        2,
    )
    keys_back, values_back = (
        lax.all_gather(key_b, "seq", axis=1, tiled=True),
        lax.all_gather(value_b, "seq", axis=1, tiled=True),
    )
    dquery = jnp.zeros((rows, group, HEADS, head), jnp.float32)
    dkey_blocks = []
    dvalue_blocks = []
    for block in range(seq_count):
        key_piece = keys_back[:, block * group : (block + 1) * group]
        value_piece = values_back[:, block * group : (block + 1) * group]
        key_seg = seg_index(seg_starts, block * group + jnp.arange(group, dtype=jnp.int32))
        scores, mask = masked_scores(query4, key_piece, query_seg, key_seg, head, scale)
        probs = jnp.where(mask, jnp.exp(scores - lse[..., None]), 0.0)
        key4 = key_piece.reshape(rows, group, HEADS, head)
        value4 = value_piece.reshape(rows, group, HEADS, head)
        dprobs = jnp.einsum("rqhd,rkhd->rhqk", dattn4, value4, preferred_element_type=jnp.float32)
        dscores = (probs * (dprobs - delta[..., None])).astype(jnp.bfloat16)
        dquery = (
            dquery
            + jnp.einsum("rhqk,rkhd->rqhd", dscores, key4, preferred_element_type=jnp.float32)
            * scale
        )
        dkey_blocks.append(
            (
                jnp.einsum("rhqk,rqhd->rkhd", dscores, query4, preferred_element_type=jnp.float32)
                * scale
            ).reshape(rows, group, width)
        )
        dvalue_blocks.append(
            jnp.einsum(
                "rhqk,rqhd->rkhd",
                probs.astype(jnp.bfloat16),
                dattn4,
                preferred_element_type=jnp.float32,
            ).reshape(rows, group, width)
        )
    dkey_all = jnp.concatenate(dkey_blocks, axis=1)
    dvalue_all = jnp.concatenate(dvalue_blocks, axis=1)
    dkey, dvalue = (
        lax.psum_scatter(
            dkey_all.astype(jnp.bfloat16), "seq", scatter_dimension=1, tiled=True
        ).astype(jnp.float32),
        lax.psum_scatter(
            dvalue_all.astype(jnp.bfloat16), "seq", scatter_dimension=1, tiled=True
        ).astype(jnp.float32),
    )
    dquery_b = dquery.reshape(rows, group, width).astype(jnp.bfloat16)
    dqkv = jnp.concatenate(
        [dquery_b, dkey.astype(jnp.bfloat16), dvalue.astype(jnp.bfloat16)], axis=-1
    )
    grad_w_qkv = outer_sum(tokens, dqkv)
    grad_b_query = column_sum(dquery_b)
    grad_b_value = column_sum(dqkv[..., 2 * width :])
    grad_tokens = (dh1 + jnp.dot(dqkv, w_qkv.T, preferred_element_type=jnp.float32)).astype(
        jnp.bfloat16
    )
    locals_list = [
        grad_w_qkv,
        grad_b_query,
        grad_b_value,
        grad_w_out,
        grad_b_out,
        grad_gain_one,
        grad_beta_one,
        grad_w_up,
        grad_b_up,
        grad_w_down,
        grad_b_down,
        grad_gain_two,
        grad_beta_two,
    ]
    flat = jnp.concatenate([piece.reshape(-1) for piece in locals_list])
    devices_all = lax.axis_size("dp") * seq_count
    length_flat = flat.shape[0]
    padded_len = -(-length_flat // devices_all) * devices_all
    flat = jnp.pad(flat, (0, padded_len - length_flat))
    partial_all = lax.psum_scatter(flat, ("dp", "seq"), scatter_dimension=0, tiled=True)
    summed = lax.all_gather(
        partial_all.astype(jnp.bfloat16), ("dp", "seq"), axis=0, tiled=True
    ).astype(partial_all.dtype)
    results = []
    position = 0
    for piece in locals_list:
        count = piece.size
        results.append(summed[position : position + count].reshape(piece.shape))
        position = position + count
    return (
        mixed,
        cls_rows,
        grad_tokens,
        results[0],
        results[1],
        results[2],
        results[3],
        results[4],
        results[5],
        results[6],
        results[7],
        results[8],
        results[9],
        results[10],
        results[11],
        results[12],
    )


def solution(mesh):
    in_specs = (
        P("dp", "seq", None),
        P("dp", None),
        P(),
        P(),
        P(),
        P(),
        P(),
        P(),
        P(),
        P(),
        P(),
        P(),
        P(),
        P(),
        P(),
        P("dp", "seq", None),
    )
    out_specs = (
        P("dp", "seq", None),
        P("dp", None, "seq"),
        P("dp", "seq", None),
        P(),
        P(),
        P(),
        P(),
        P(),
        P(),
        P(),
        P(),
        P(),
        P(),
        P(),
        P(),
        P(),
    )
    return jax.shard_map(
        on_device, mesh=mesh, in_specs=in_specs, out_specs=out_specs, check_vma=False
    )
```

profile of v0, /device:TPU:0, one launch (start us, length us, event | category | flops | bytes accessed | tf_op | source)
XLA Modules:
  0.0 1445.1 jit_solution(16769771641847974704)
XLA Ops:
  24.1 57.7 %all-gather.3.cloned.1.call-done = bf16[2,1024,768]{2,1,0:T(8,128)(2,1)} async-done(((bf16[2,256,768]{2,1,0:T(8,128)(2,1)}), bf16[2,1024,768]{2,1,0:T(8,128)(2,1)}) %all-gather.3.cloned.1.call-update) | async-done | bytes 3145744 | tf_op jit(solution)/shard_map/all_gather | solution.py:79
  86.5 14.9 %fusion = (f32[2,12,256]{2,1,0:T(8,128)S(1)}, f32[2,12,256,1024]{3,2,1,0:T(8,128)}) fusion(pred[2,256,1024]{2,1,0:T(8,128)(4,1)} %broadcast_compare_fusion, bf16[2,256,12,64]{1,3,2,0:T(8,128)(2,1)} %bitcast.154, bf16[2,1024,12,64]{1,3,2,0:T(8,128)(2,1)} %bitcast.164), kind=kOutput, calls=%fused_computation.2 | convolution fusion | flops 824174592 | bytes 29646848 | tf_op jit(solution)/shard_map/rqhd,rkhd->rhqk/dot_general | solution.py:44
  101.4 12.7 fusion.1
  115.4 30.8 %all-gather.5.cloned.1.call-done = bf16[2,1024,768]{2,1,0:T(8,128)(2,1)} async-done(((bf16[2,256,768]{2,1,0:T(8,128)(2,1)}), bf16[2,1024,768]{2,1,0:T(8,128)(2,1)}) %all-gather.5.cloned.1.call-update) | async-done | bytes 3145744 | tf_op jit(solution)/shard_map/all_gather | solution.py:80
  150.8 14.1 fusion.48
  171.2 7.2 fusion.50
  178.4 14.6 %multiply_convert_fusion.4 = (bf16[2,256,3072]{2,1,0:T(8,128)(2,1)S(1)}, f32[2,256,3072]{2,1,0:T(8,128)S(1)}) fusion(f32[2,256,3072]{2,1,0:T(8,128)S(1)} %get-tuple-element.72, f32[3072]{0:T(1024)S(1)} %copy-done.36, u8[256,3072]{1,0:T(8,128)(4,1)S(1)} %get-tuple-element.17, u8[256,3072]{1,0:T(8,128)(4,1)S(1)} %get-tuple-element.16), kind=kLoop, calls=%fused_computation.24 | loop fusion | flops 111673344 | bytes 17313792 | tf_op jit(solution)/shard_map/convert_element_type | solution.py:110
  193.1 6.3 fusion.108
  203.7 9.0 convert_reduce_fusion
  212.7 7.7 multiply_reduce_fusion
  318.0 5.5 fusion.59
  325.8 5.4 fusion.62
  333.5 5.5 fusion.65
  341.3 5.4 fusion.68
  371.3 5.4 convolution_bitcast_fusion.2
  376.7 6.0 copy.167
  387.8 10.8 reshape.320
  404.6 35.1 %reduce-scatter.8.cloned.1.call-done = bf16[2,256,768]{2,1,0:T(8,128)(2,1)} async-done(((bf16[2,1024,768]{2,1,0:T(8,128)(2,1)}), bf16[2,256,768]{2,1,0:T(8,128)(2,1)}) %reduce-scatter.8.cloned.1.call-update) | async-done | bytes 786448 | tf_op jit(solution)/shard_map/reduce_scatter | solution.py:183
  439.7 6.8 convolution_bitcast_fusion
  446.5 8.0 copy.158
  454.5 7.9 reshape.317
  470.4 21.3 %dynamic-update-slice.4 = f32[7087104]{0:T(1024)} dynamic-update-slice(f32[7087104]{0:T(1024)} %constant_dynamic-update-slice_fusion.7, f32[589824]{0:T(1024)} %reshape.318, s32[]{} %constant.113) | dynamic-update-slice | bytes 4718596
  495.6 80.6 %dynamic-update-slice.8 = f32[7087104]{0:T(1024)} dynamic-update-slice(f32[7087104]{0:T(1024)} %constant_dynamic-update-slice_fusion.4, f32[2359296]{0:T(1024)} %bitcast.163, s32[]{} %constant.117) | dynamic-update-slice | bytes 18874372
  577.5 80.3 %dynamic-update-slice.10 = f32[7087104]{0:T(1024)} dynamic-update-slice(f32[7087104]{0:T(1024)} %constant_dynamic-update-slice_fusion.3, f32[2359296]{0:T(1024)} %reshape.320, s32[]{} %constant.119) | dynamic-update-slice | bytes 18874372
  661.7 458.3 %all-reduce.6 = bf16[7087104]{0:T(1024)(128)(2,1)} all-reduce(f32[7087104]{0:T(1024)} %constant_dynamic-update-slice_fusion), channel_id=5, replica_groups=mesh['dp'=8,'seq'=4] {'dp','seq'}, use_global_device_ids=true, to_apply=%region_29.30.clone | all-reduce | flops 7087104 | bytes 42522624
  1127.4 7.7 dynamic-update-slice
  1138.2 5.5 add_convert_fusion.1
  1143.7 240.3 %all-reduce.5.cloned.1.call-done = bf16[7087104]{0:T(1024)(128)(2,1)} async-done(((bf16[7087104]{0:T(1024)(128)(2,1)}), bf16[7087104]{0:T(1024)(128)(2,1)}) %all-reduce.5.cloned.1.call-update) | async-done | bytes 14174224
  1384.0 10.0 fusion.104
  1394.0 10.9 reshape.321
  1404.9 11.3 slice.126
  1420.7 8.2 slice.115
  (221 shorter events, 218.8 us)
Async XLA Ops:
  7.2 8.4 copy-start.45
  7.2 8.4 copy-start.46
  7.2 74.6 %all-gather.3.cloned.1.call-start = ((), (), s32[]{:S(2)}) async-start(), calls=%async_computation.3 | async-start | bytes 3932160 | tf_op jit(solution)/shard_map/all_gather | solution.py:79
  14.5 6.7 copy-start.38
  15.5 130.6 %all-gather.5.cloned.1.call-start = ((), (), s32[]{:S(2)}) async-start(), calls=%async_computation.4 | async-start | bytes 3932160 | tf_op jit(solution)/shard_map/all_gather | solution.py:80
  18.9 385.7 %reduce-scatter.6.cloned.1.call-start = ((), (), s32[]{:S(2)}) async-start(), calls=%async_computation.5 | async-start | bytes 3932160 | tf_op jit(solution)/shard_map/reduce_scatter | solution.py:180
  86.4 15.0 %copy-start.21 = (pred[2,256,1024]{2,1,0:T(8,128)(4,1)S(1)}, pred[2,256,1024]{2,1,0:T(8,128)(4,1)}, u32[]{:S(2)}) copy-start(pred[2,256,1024]{2,1,0:T(8,128)(4,1)} %broadcast_compare_fusion) | copy-start | bytes 1572868
  101.4 12.7 copy-start.29
  150.8 17.1 %copy-start.51 = (f32[768]{0:T(1024)S(1)}, f32[768]{0:T(1024)}, u32[]{:S(2)}) copy-start(f32[768]{0:T(1024)} %param.22) | copy-start | bytes 9220
  170.8 22.2 %copy-start.17 = (f32[2,256,768]{2,1,0:T(8,128)}, f32[2,256,768]{2,1,0:T(8,128)S(1)}, u32[]{:S(2)}) copy-start(f32[2,256,768]{2,1,0:T(8,128)S(1)} %get-tuple-element.71) | copy-start | bytes 4718596
  171.2 49.2 %copy-start.42 = (f32[2,256]{1,0:T(2,128)}, f32[2,256]{1,0:T(2,128)S(1)}, u32[]{:S(2)}) copy-start(f32[2,256]{1,0:T(2,128)S(1)} %fusion.81) | copy-start | bytes 6148
  171.2 7.2 copy-start.36
  178.4 14.6 %copy-start.52 = (f32[768]{0:T(1024)S(1)}, f32[768]{0:T(1024)}, u32[]{:S(2)}) copy-start(f32[768]{0:T(1024)} %param.28) | copy-start | bytes 9220
  193.0 6.3 copy-start.23
  193.1 6.3 copy-start.13
  193.1 6.3 copy-start.31
  193.1 8.4 copy-start.47
  203.7 9.0 copy-start.27
  212.7 7.8 copy-start.18
  317.6 122.1 %reduce-scatter.8.cloned.1.call-start = ((), (), s32[]{:S(2)}) async-start(), calls=%async_computation.6 | async-start | bytes 3932160 | tf_op jit(solution)/shard_map/reduce_scatter | solution.py:183
  352.2 782.9 %reduce-scatter.10.cloned.1.call-start = ((), (), s32[]{:S(2)}) async-start(), calls=%async_computation.8 | async-start | bytes 245760
  364.2 7.0 copy-start.50
  364.2 7.0 copy-start.54
  387.8 10.8 copy-start.39
  387.8 10.8 copy-start.41
  404.3 979.7 %all-reduce.5.cloned.1.call-start = ((), (), s32[]{:S(2)}) async-start(), calls=%async_computation.7 | async-start | bytes 28348416
  462.4 6.5 copy-start.26
  462.4 29.2 %copy-start.34 = (f32[768]{0:T(1024)S(1)}, f32[768]{0:T(1024)}, u32[]{:S(2)}) copy-start(f32[768]{0:T(1024)} %get-tuple-element.33) | copy-start | bytes 9220
  462.4 31.8 %copy-start.48 = (f32[768]{0:T(1024)S(1)}, f32[768]{0:T(1024)}, u32[]{:S(2)}) copy-start(f32[768]{0:T(1024)} %get-tuple-element.24) | copy-start | bytes 9220
  495.6 80.6 %copy-start.37 = (f32[3072]{0:T(1024)S(1)}, f32[3072]{0:T(1024)}, u32[]{:S(2)}) copy-start(f32[3072]{0:T(1024)} %get-tuple-element.80) | copy-start | bytes 36868
  577.5 80.3 %copy-start.33 = (f32[768]{0:T(1024)S(1)}, f32[768]{0:T(1024)}, u32[]{:S(2)}) copy-start(f32[768]{0:T(1024)} %get-tuple-element.31) | copy-start | bytes 9220
  577.5 81.6 %copy-start.32 = (f32[768]{0:T(1024)S(1)}, f32[768]{0:T(1024)}, u32[]{:S(2)}) copy-start(f32[768]{0:T(1024)} %get-tuple-element.20) | copy-start | bytes 9220
  (29 other events, 107.3 us)
Sparse Core Ops, SparseCore 0:
  15.6 66.1 all-gather.2
  84.0 62.1 all-gather.4
  317.7 58.9 reduce-scatter.5
  379.4 60.2 reduce-scatter.7
  442.4 19.4 reduce-scatter.9
  1135.2 248.7 all-reduce.4
where the time goes:
time: 1470 us; the launch traced here: 1450 us
  blocking collectives  458 us (31%)
  local copies, waits for them, and re-layouts  383 us (26%)
  waiting for transfers between devices  364 us (25%)
  matrix products  176 us (12%)
  other arithmetic  48.3 us (3%)
  between operations  15.1 us (1%)
    unnamed x1, blocking collectives  458 us
    unnamed x8, waiting for transfers between devices  240 us
    unnamed x130, local copies, waits for them, and re-layouts  232 us
    all_gather x1, waiting for transfers between devices, on_device(): add_key_piece = lax.all_gather(key_b, 'seq', axis=1, tiled=True)  57.7 us
    slice x8, local copies, waits for them, and re-layouts, on_device(): results.append(summed[position:position + count].reshape(piece.shape))  43 us
    dot_general x5, matrix products, masked_scores(): jnp.einsum('rqhd,rkhd->rhqk', query4, key4, preferred_element_type=jnp.fl...  35.5 us
    reduce_scatter x1, waiting for transfers between devices, on_device(): lax.psum_scatter(dvalue_all.astype(jnp.bfloat16), 'seq', scatter_dimensio...  35.1 us
    all_gather x1, waiting for transfers between devices, on_device(): add_value_piece = lax.all_gather(value_b, 'seq', axis=1, tiled=True)  30.8 us
  transfers between devices with their start and end apart: 6, of which 4 were waited for; matrix products, arithmetic and copies ran while one was open for 26% of the time, Pallas kernels for 0%

commit v1 on v0

v1 whole, which is shorter than its diff:
```python
from functools import partial

import jax
import jax.numpy as jnp
from jax import lax
from jax.experimental import pallas as pl
from jax.experimental.pallas import tpu as pltpu
from jax.sharding import PartitionSpec as P

HEADS = 12
LINE = ("core", "seq")
F32, BF16 = jnp.float32, jnp.bfloat16
NT = (((1,), (1,)), ((), ()))
TN = (((0,), (0,)), ((), ()))
NEGATIVE = -1e30
MIB = 1 << 20


def dot(a, b, dims=(((1,), (0,)), ((), ()))):
    return lax.dot_general(a, b, dims, preferred_element_type=F32)


def whole(shape):
    return pl.BlockSpec(shape, lambda *_: (0,) * len(shape))


def call(body, grid, in_specs, out_specs, out_shape, scratch, flops, moved, vmem, ids=None):
    params = pltpu.CompilerParams(
        dimension_semantics=("arbitrary",) * len(grid), vmem_limit_bytes=vmem * MIB
    )
    return pl.pallas_call(
        body,
        grid_spec=pltpu.PrefetchScalarGridSpec(
            num_scalar_prefetch=0 if ids is None else 1,
            grid=grid,
            in_specs=in_specs,
            out_specs=out_specs,
            scratch_shapes=scratch,
        ),
        out_shape=out_shape,
        compiler_params=params,
        cost_estimate=pl.CostEstimate(flops=flops, bytes_accessed=moved, transcendentals=0),
    )


def struct(shape, kind):
    return jax.ShapeDtypeStruct(shape, kind)


def attend_body(
    x_ref, wq_ref, wk_ref, wv_ref, bq_ref, bv_ref, qhot_ref, khot_ref,
    q_ref, k_ref, v_ref, attn_ref, lse_ref,
):
    count = q_ref.shape[0]
    x = x_ref[...]
    q = ((dot(x[:count], wq_ref[...]) + bq_ref[...]).astype(BF16).astype(F32) * 0.125).astype(BF16)
    k = dot(x, wk_ref[...]).astype(BF16)
    v = (dot(x, wv_ref[...]) + bv_ref[...]).astype(BF16)
    q_ref[...] = q
    k_ref[...] = k
    v_ref[...] = v
    lane = lax.broadcasted_iota(jnp.int32, (1, 128), 1)
    lane_q = lax.broadcasted_iota(jnp.int32, (count, 128), 1)
    lse = jnp.zeros((count, 128), F32)
    ones = jnp.ones(khot_ref.shape, BF16)
    for pair in range(2):
        part = slice(128 * pair, 128 * pair + 128)
        keys = jnp.concatenate([k[:, part], khot_ref[...]], axis=1)
        attn = jnp.zeros((count, 128), F32)
        for side in range(2):
            mine = ((lane >= 64) == (side == 1)).astype(F32).astype(BF16)
            queries = jnp.concatenate([q[:, part] * mine, qhot_ref[...]], axis=1)
            scores = dot(queries, keys, NT)
            high = jnp.max(scores, axis=1, keepdims=True)
            weights = jnp.exp(scores - high).astype(BF16)
            values = jnp.concatenate([v[:, part] * mine, ones], axis=1)
            both = dot(weights, values)
            total = both[:, 128:]
            attn = attn + both[:, :128] / total
            lse = jnp.where(lane_q == 2 * pair + side, high + jnp.log(total), lse)
        attn_ref[:, part] = attn
    lse_ref[0] = jnp.transpose(lse)[:8]


def attend(x_all, w_qkv, b_query, b_value, qhot, khot):
    keys, width = x_all.shape
    count = qhot.shape[0]
    quads = width // 256
    weight = [pl.BlockSpec((width, 256), lambda i, n=n: (0, n * quads + i)) for n in range(3)]
    column = lambda rows: pl.BlockSpec((rows, 256), lambda i: (0, i))
    return call(
        attend_body,
        (quads,),
        [whole(x_all.shape), *weight, column(1), column(1), whole(qhot.shape), whole(khot.shape)],
        [column(count), column(keys), column(keys), column(count), pl.BlockSpec((1, 8, count), lambda i: (i, 0, 0))],
        [
            struct((count, width), BF16),
            struct((keys, width), BF16),
            struct((keys, width), BF16),
            struct((count, width), F32),
            struct((quads, 8, count), F32),
        ],
        [],
        13_000_000_000,
        16_000_000,
        56,
    )(x_all, w_qkv, w_qkv, w_qkv, b_query, b_value, qhot, khot)


def centre(h):
    mean = jnp.mean(h, axis=-1, keepdims=True)
    cent = h - mean
    inv = lax.rsqrt(jnp.mean(cent * cent, axis=-1, keepdims=True) + 1e-06)
    return cent * inv, inv


def norm_back(cot, unit, inv, gain):
    g = cot * gain
    return inv * (
        g - jnp.mean(g, axis=-1, keepdims=True) - unit * jnp.mean(g * unit, axis=-1, keepdims=True)
    )


def row_sum(values):
    return jnp.sum(values, axis=0, keepdims=True)


UP_STEPS = 6
CHUNKS = 8


def forward_body(
    ids, x_ref, attn_ref, wo_ref, bo_ref, g1_ref, e1_ref, wu_ref, bu_ref, wd_ref, bd_ref, g2_ref, e2_ref, cot0_ref, cot1_ref,
    mixed0_ref, mixed1_ref, n1_ref, unit_ref, inv_ref, slope_ref, dh2_ref, dffn_ref, vec_ref, send_ref, keep_ref,
    full, sums, acts,
):
    step = pl.program_id(0)
    part = wu_ref.shape[1]

    @pl.when(step == 0)
    def _():
        branch = dot(attn_ref[...].astype(BF16), wo_ref[...]) + bo_ref[...]
        unit, inv = centre(x_ref[...].astype(F32) + branch)
        n1 = unit * g1_ref[...] + e1_ref[...]
        unit_ref[...] = unit
        inv_ref[...] = jnp.broadcast_to(inv, inv_ref.shape)
        full[...] = n1
        n1_ref[...] = n1.astype(BF16)
        sums[...] = jnp.zeros_like(sums)

    @pl.when(step < UP_STEPS)
    def _():
        pre = dot(n1_ref[...], wu_ref[...]) + bu_ref[...]
        phi = 0.5 * (1.0 + lax.erf(pre * 0.7071067811865476))
        slope = phi + pre * (jnp.exp(-0.5 * pre * pre) * 0.3989422804014327)
        slope_ref[...] = slope.astype(BF16)
        act = (pre * phi).astype(BF16)
        acts[:, pl.ds(pl.multiple_of(step * part, part), part)] = act
        sums[...] += dot(act, wd_ref[...])

    @pl.when(step == UP_STEPS - 1)
    def _():
        h2 = full[...] + sums[...] + bd_ref[...]
        unit, inv = centre(h2)
        cot = jnp.concatenate([cot0_ref[...], cot1_ref[...]], axis=0).astype(F32)
        mixed = (unit * g2_ref[...] + e2_ref[...]).astype(BF16)
        half = mixed0_ref.shape[0]
        mixed0_ref[...] = mixed[:half]
        mixed1_ref[...] = mixed[half:]
        dh2 = norm_back(cot, unit, inv, g2_ref[...])
        dh2_ref[...] = dh2
        dffn = dh2.astype(BF16)
        dffn_ref[...] = dffn
        vec_ref[...] = jnp.concatenate(
            [
                row_sum(cot * unit),
                row_sum(cot),
                row_sum(dffn.astype(F32)),
                jnp.zeros((5, cot.shape[1]), F32),
            ],
            axis=0,
        )

    @pl.when(step >= UP_STEPS)
    def _():
        chunk = ((step - UP_STEPS) ^ 4) ^ (ids[0] >> 2)
        grad = dot(acts[:, pl.ds(pl.multiple_of(chunk * 384, 384), 384)], dffn_ref[...], TN)
        grad = grad.astype(BF16)
        rows = grad.shape[0] // 4

        @pl.when(step < UP_STEPS + 4)
        def _():
            for i in range(4):
                send_ref[(ids[0] & 3) ^ i] = grad[i * rows : (i + 1) * rows]

        @pl.when(step >= UP_STEPS + 4)
        def _():
            for i in range(4):
                keep_ref[(ids[0] & 3) ^ i] = grad[i * rows : (i + 1) * rows]


def forward(ids, x_all, attn, w_out, b_out, g1, e1, w_up, b_up, w_down, b_down, g2, e2, cot):
    count, width = attn.shape
    half = (count // 2, width)
    hidden = w_up.shape[1]
    part = hidden // UP_STEPS
    up = lambda s, *_: (0, jnp.minimum(s, UP_STEPS - 1))
    down = lambda s, *_: (jnp.minimum(s, UP_STEPS - 1), 0)
    line = whole((1, width))
    block = (4, hidden // 32, width)
    return call(
        forward_body,
        (UP_STEPS + CHUNKS,),
        [
            whole((count, width)), whole((count, width)), whole((width, width)), line, line, line,
            pl.BlockSpec((width, part), up), pl.BlockSpec((1, part), up), pl.BlockSpec((part, width), down),
            line, line, line, whole(half), whole(half),
        ],
        [
            whole(half), whole(half), whole((count, width)), whole((count, width)), whole((count, 128)),
            pl.BlockSpec((count, part), up), whole((count, width)), whole((count, width)), whole((8, width)),
            pl.BlockSpec(block, lambda s, *_: (jnp.clip(s - UP_STEPS, 0, 3), 0, 0)),
            pl.BlockSpec(block, lambda s, *_: (jnp.clip(s - UP_STEPS - 4, 0, 3), 0, 0)),
        ],
        [
            struct(half, BF16), struct(half, BF16), struct((count, width), BF16), struct((count, width), F32),
            struct((count, 128), F32), struct((count, hidden), BF16), struct((count, width), F32),
            struct((count, width), BF16), struct((8, width), F32),
            struct((16, hidden // 32, width), BF16), struct((16, hidden // 32, width), BF16),
        ],
        [pltpu.VMEM((count, width), F32), pltpu.VMEM((count, width), F32), pltpu.VMEM((count, hidden), BF16)],
        8_000_000_000,
        30_000_000,
        56,
        ids,
    )(ids, x_all, attn, w_out, b_out, g1, e1, w_up, b_up, w_down, b_down, g2, e2, *cot)


def back_step(ids, dffn_ref, wd_ref, wu_ref, slope_ref, n1_ref, out_ref, bu_ref, sums):
    dact = dot(dffn_ref[...], wd_ref[...], NT)
    dpre = (dact * slope_ref[...].astype(F32)).astype(BF16)
    bu_ref[...] = jnp.broadcast_to(row_sum(dpre.astype(F32))[None], bu_ref.shape)
    sums[...] += dot(dpre, wu_ref[...], NT)
    grad = dot(n1_ref[...], dpre, TN).astype(BF16)
    rows, part = out_ref.shape[1], dpre.shape[1]
    for i in range(4):
        block = (ids[1] & 3) ^ i
        at = 2 * i * rows
        out_ref[block, :, :part] = grad[at : at + rows]
        out_ref[block, :, part:] = grad[at + rows : at + 2 * rows]


def back_send_body(ids, dffn_ref, wd_ref, wu_ref, slope_ref, n1_ref, dh2_ref, out_ref, bu_ref, sum_ref):
    step = pl.program_id(0)

    @pl.when(step == 0)
    def _():
        sum_ref[...] = dh2_ref[...]

    back_step(ids, dffn_ref, wd_ref, wu_ref, slope_ref, n1_ref, out_ref, bu_ref, sum_ref)


def place_rows(ids, which, grads, send_ref, keep_ref):
    rows, part = keep_ref.shape[1:]
    core, mine = ids[0] >> 4, ids[which] & 15
    for side, ref in ((core, keep_ref), (1 - core, send_ref)):
        at = pl.multiple_of(side * part, 128)

        def place(j, carry, at=at, ref=ref):
            from_row = pl.multiple_of((j ^ mine) * rows, 16)
            ref[j] = grads[pl.ds(from_row, rows), pl.ds(at, part)]
            return carry

        lax.fori_loop(0, 16, place, 0)


def back_keep_body(
    ids, dffn_ref, wd_ref, wu_ref, slope_ref, n1_ref, part_ref, unit_ref, inv_ref, g1_ref, attn_ref, wo_ref,
    out_ref, bu_ref, dh1_ref, dattn_ref, osend_ref, okeep_ref, vec_ref,
    sums, grads,
):
    step = pl.program_id(0)

    @pl.when(step == 0)
    def _():
        sums[...] = part_ref[...]

    back_step(ids, dffn_ref, wd_ref, wu_ref, slope_ref, n1_ref, out_ref, bu_ref, sums)

    @pl.when(step == 3)
    def _():
        dn1 = sums[...]
        unit = unit_ref[...]
        dh1 = norm_back(dn1, unit, inv_ref[:, :1], g1_ref[...])
        dh1_ref[...] = dh1
        dbranch = dh1.astype(BF16)
        dattn_ref[...] = dot(dbranch, wo_ref[...], NT).astype(BF16)
        grads[...] = dot(attn_ref[...].astype(BF16), dbranch, TN).astype(BF16)
        place_rows(ids, 0, grads, osend_ref, okeep_ref)
        vec_ref[...] = jnp.concatenate(
            [
                row_sum(dn1 * unit),
                row_sum(dn1),
                row_sum(dbranch.astype(F32)),
                jnp.zeros((5, dn1.shape[1]), F32),
            ],
            axis=0,
        )


def back(first, ids, dffn, w_down, w_up, slope, n1, *more):
    count, width = dffn.shape
    hidden = w_up.shape[1]
    part = hidden // CHUNKS
    true = lambda s, ids: s ^ first ^ (ids[1] >> 2)
    piece = (16, width // 8, 2 * part)
    full = whole((count, width))
    in_specs = [
        full,
        pl.BlockSpec((part, width), lambda s, ids: (true(s, ids), 0)),
        pl.BlockSpec((width, part), lambda s, ids: (0, true(s, ids))),
        pl.BlockSpec((count, part), lambda s, ids: (0, true(s, ids))),
        full, full,
    ]
    out_specs = [pl.BlockSpec((4, *piece[1:]), lambda s, ids: (s, 0, 0)), pl.BlockSpec((1, 8, part), lambda s, ids: ((true(s, ids)) & 3, 0, 0))]
    out_shape = [struct(piece, BF16), struct((4, 8, part), F32)]
    if first:
        out_specs += [full]
        out_shape += [struct((count, width), F32)]
        body, scratch = back_send_body, []
    else:
        in_specs += [full, whole((count, 128)), whole((1, width)), full, whole((width, width))]
        small = (16, width // 16, width // 2)
        out_specs += [full, full, whole(small), whole(small), whole((8, width))]
        out_shape += [
            struct((count, width), F32), struct((count, width), BF16), struct(small, BF16), struct(small, BF16),
            struct((8, width), F32),
        ]
        body, scratch = back_keep_body, [pltpu.VMEM((count, width), F32), pltpu.VMEM((width, width), BF16)]
    return call(
        body, (4,), in_specs, out_specs, out_shape, scratch, 5_000_000_000, 16_000_000, 56, ids
    )(ids, dffn, w_down, w_up, slope, n1, *more)


def attend_back_body(
    quad, ids, x_ref, q_ref, k_ref, v_ref, dattn_ref, attn_ref, lse_ref, qhot_ref, khot_ref,
    send_ref, keep_ref, dq_ref, dk_ref, dv_ref, vec_ref,
    grads, dqs, dks, dvs,
):
    count = q_ref.shape[0]
    lane = lax.broadcasted_iota(jnp.int32, (1, 128), 1)

    dqs[...] = jnp.zeros_like(dqs)
    dks[...] = jnp.zeros_like(dks)
    dvs[...] = jnp.zeros_like(dvs)

    def one_head(head, carry):
        part = pl.ds(pl.multiple_of((head >> 1) * 128, 128), 128)
        mine = ((lane >> 6) == (head & 1)).astype(F32)
        k, do = k_ref[:, part], dattn_ref[:, part]
        delta = row_sum(jnp.transpose(do.astype(F32) * attn_ref[:, part] * mine))
        mine = mine.astype(BF16)
        queries = q_ref[:, part] * mine
        douts = do * mine
        keys = jnp.concatenate([k, khot_ref[...]], axis=1)
        scores = dot(keys, jnp.concatenate([queries, qhot_ref[...]], axis=1), NT)
        probs = jnp.exp(scores - lse_ref[0, pl.ds(head, 1)])
        dprobs = dot(v_ref[:, part], douts, NT)
        dscores = (probs * (dprobs - delta)).astype(BF16)
        dvs[:, part] += dot(probs.astype(BF16), douts)
        dks[:, part] += dot(dscores, queries)
        dqs[:, part] += dot(dscores, k * mine, TN)
        return carry

    lax.fori_loop(0, 4, one_head, 0)
    dq = (dqs[...] * 0.125).astype(BF16)
    dk = dks[...].astype(BF16)
    dv = dvs[...].astype(BF16)
    vec_ref[...] = jnp.concatenate(
        [row_sum(dq.astype(F32)), row_sum(dv.astype(F32)), jnp.zeros((6, 256), F32)], axis=0
    )
    x = x_ref[...]
    for n, (left, right) in enumerate(((x[:count], dq), (x, dk), (x, dv))):
        grads[:, 256 * n : 256 * n + 256] = dot(left, right, TN).astype(BF16)
    dq_ref[...] = dq
    dk_ref[...] = dk
    dv_ref[...] = dv
    place_rows(ids, 1 if quad else 0, grads, send_ref, keep_ref)


def attend_back(quad, ids, x_all, q, k, v, dattn, attn, lse, qhot, khot):
    keys, width = x_all.shape
    count = q.shape[0]
    column = lambda rows: pl.BlockSpec((rows, 256), lambda i, ids: (0, quad))
    piece = (16, width // 16, width // 2)
    return call(
        partial(attend_back_body, quad),
        (1,),
        [
            whole(x_all.shape), column(count), column(keys), column(keys), column(count), column(count),
            pl.BlockSpec((1, 8, count), lambda i, ids: (quad, 0, 0)), whole(qhot.shape), whole(khot.shape),
        ],
        [whole(piece)] * 2 + [whole((count, 256)), whole((keys, 256)), whole((keys, 256)), whole((8, 256))],
        [struct(piece, BF16)] * 2
        + [
            struct((count, 256), BF16), struct((keys, 256), BF16), struct((keys, 256), BF16),
            struct((8, 256), F32),
        ],
        [
            pltpu.VMEM((width, width), BF16), pltpu.VMEM((count, 256), F32),
            pltpu.VMEM((keys, 256), F32), pltpu.VMEM((keys, 256), F32),
        ],
        12_000_000_000,
        10_000_000,
        58,
        ids,
    )(ids, x_all, q, k, v, dattn, attn, lse, qhot, khot)


def tokens_back_body(*refs):
    dqs, dks, dvs = refs[:3], refs[3:6], refs[6:9]
    w_ref, dh1_ref, own_ref, there_ref = refs[9:]
    count, width = dh1_ref.shape
    own, there = dh1_ref[...], None
    for quad in range(3):
        wq, wk, wv = (w_ref[:, n * width + 256 * quad : n * width + 256 * quad + 256] for n in range(3))
        dk, dv = dks[quad][...], dvs[quad][...]
        own = own + (dot(dqs[quad][...], wq, NT) + dot(dk[:count], wk, NT) + dot(dv[:count], wv, NT))
        rest = dot(dk[count:], wk, NT) + dot(dv[count:], wv, NT)
        there = rest if there is None else there + rest
    own_ref[...] = own
    there_ref[...] = there.astype(BF16)


def tokens_back(dqs, dks, dvs, w_qkv, dh1):
    operands = (*dqs, *dks, *dvs, w_qkv, dh1)
    return call(
        tokens_back_body,
        (1,),
        [whole(a.shape) for a in operands],
        [whole(dh1.shape)] * 2,
        [struct(dh1.shape, F32), struct(dh1.shape, BF16)],
        [],
        6_000_000_000,
        12_000_000,
        56,
    )(*operands)


def unfold_down_body(ids, own_ref, other_ref, out_ref):
    step = pl.program_id(0)
    rows = own_ref.shape[1]
    for half, ref in enumerate((own_ref, other_ref)):

        @pl.when(step // 4 == half)
        def _(ref=ref):
            for i in range(4):
                out_ref[i * rows : (i + 1) * rows] = ref[(ids[0] & 3) ^ i].astype(F32)


def unfold_down(ids, own, other, shape):
    _, rows, columns = own.shape
    block = (4, rows, columns)
    return call(
        unfold_down_body,
        (CHUNKS,),
        [
            pl.BlockSpec(block, lambda s, ids: (jnp.minimum(s, 3), 0, 0)),
            pl.BlockSpec(block, lambda s, ids: (jnp.maximum(s - 4, 0), 0, 0)),
        ],
        pl.BlockSpec((4 * rows, columns), lambda s, ids: (s ^ (ids[0] >> 2), 0)),
        struct(shape, F32),
        [],
        0,
        16_000_000,
        32,
        ids,
    )(ids, own, other)


def unfold_up_body(ids, own_ref, other_ref, out_ref):
    step = pl.program_id(0)
    rows, part = own_ref.shape[1], out_ref.shape[1]
    for half, ref in enumerate((own_ref, other_ref)):

        @pl.when(step // 4 == half)
        def _(ref=ref):
            for i in range(4):
                at = 2 * i * rows
                block = ref[(ids[1] & 3) ^ i].astype(F32)
                out_ref[at : at + rows] = block[:, :part]
                out_ref[at + rows : at + 2 * rows] = block[:, part:]


def unfold_up(ids, own, other, shape):
    _, rows, columns = own.shape
    block = (4, rows, columns)
    return call(
        unfold_up_body,
        (CHUNKS,),
        [
            pl.BlockSpec(block, lambda s, ids: (jnp.minimum(s, 3), 0, 0)),
            pl.BlockSpec(block, lambda s, ids: (jnp.maximum(s - 4, 0), 0, 0)),
        ],
        pl.BlockSpec((8 * rows, columns // 2), lambda s, ids: (0, s ^ (ids[1] >> 2))),
        struct(shape, F32),
        [],
        0,
        16_000_000,
        32,
        ids,
    )(ids, own, other)


def unfold_two_body(ids, a_own, a_other, b_own, b_other, qkv_ref, out_ref):
    rows = a_own.shape[1]
    for core in range(2):

        @pl.when((ids[2] >> 4) == core)
        def _(core=core):
            for i in range(4):
                at = slice(i * rows, (i + 1) * rows)
                for half, a, b in ((core, a_own, b_own), (1 - core, a_other, b_other)):
                    a = a[(ids[2] & 3) ^ i].astype(F32)
                    b = b[(ids[3] & 3) ^ i].astype(F32)
                    for quad, grad in enumerate((a[:, :384], b[:, :384], b[:, 384:])):
                        col = 256 * quad
                        if half == 0:
                            qkv_ref[at, col : col + 256] = grad[:, :256]
                            qkv_ref[at, 768 + col : 768 + col + 128] = grad[:, 256:]
                        else:
                            qkv_ref[at, 768 + col + 128 : 768 + col + 256] = grad[:, :128]
                            qkv_ref[at, 1536 + col : 1536 + col + 256] = grad[:, 128:]
                    out_ref[at, 384 * half : 384 * half + 384] = a[:, 384:]


def unfold_two(ids, a_own, a_other, b_own, b_other):
    _, rows, columns = a_own.shape
    width = 16 * rows
    block = (4, rows, columns)
    source = lambda n: pl.BlockSpec(block, lambda s, ids: (s ^ ((ids[n] >> 2) & 3), 0, 0))
    return call(
        unfold_two_body,
        (4,),
        [source(2), source(2), source(3), source(3)],
        [
            pl.BlockSpec((4 * rows, 3 * width), lambda s, ids: (s, 0)),
            pl.BlockSpec((4 * rows, width), lambda s, ids: (s, 0)),
        ],
        [struct((width, 3 * width), F32), struct((width, width), F32)],
        [],
        0,
        16_000_000,
        32,
        ids,
    )(ids, a_own, a_other, b_own, b_other)


class Moves:
    def __init__(self, pairs, seq_count):
        self.pairs, self.seq_count = pairs, seq_count
        devices = [(core, z) for core in range(2) for z in range(seq_count)]
        self.to_rows = []
        for k in range(2):
            self.to_rows.append(
                [
                    (core * seq_count + z, z // 2 * seq_count + 2 * core + (k ^ (z & 1)))
                    for core, z in devices
                ]
            )
        self.from_rows = [[(b, a) for a, b in perm] for perm in self.to_rows]
        self.rest = pairs // 4

    @staticmethod
    def swap(values, axis, count, bit):
        return lax.ppermute(values, axis, [(i, i ^ bit) for i in range(count)])

    def core(self, values):
        return self.swap(values, "core", 2, 1)

    def quad(self, values, bit):
        return self.swap(values, "quad", 4, bit)

    def line(self, values, bit):
        return self.swap(values, "seq", self.seq_count, bit)


def add(a, b):
    return (a.astype(F32) + b.astype(F32)).astype(BF16)


def sum_rest(moves, values):
    bit = 1
    while bit < moves.rest:
        values = values + moves.swap(values, "rest", moves.rest, bit)
        bit *= 2
    return values


class Clock:
    def __init__(self):
        self.mark, self.stopped = None, False

    def stop(self):
        self.stopped = True

    def tie(self, *values):
        if self.stopped or self.mark is None:
            return values
        return lax.optimization_barrier((*values, self.mark))[:-1]


def halve(clock, keep, got):
    keep, got = clock.tie(keep, got)
    half = keep.shape[0] // 2
    send = add(keep[half:], got[half:])
    clock.mark = send
    return add(keep[:half], got[:half]), send


def total(parts):
    return sum(part.astype(F32) for part in parts).astype(BF16)


def send_blocks(clock, parts, first, last):
    parts = list(clock.tie(*parts))
    send = total([part[first:last] for part in parts])
    clock.mark = send
    return parts, send


def halve_parts(clock, first, second):
    values = clock.tie(*first, *second)
    both = values[: len(first)], values[len(first) :]
    send = jnp.concatenate([total([p[2:4] for p in parts]) for parts in both], axis=1)
    clock.mark = send
    return jnp.concatenate([total([p[:2] for p in parts]) for parts in both], axis=1), send


def halve_wide(keep, got):
    half = keep[0].shape[0] // 2
    keeps, sends = zip(
        *((add(a[:half], b[:half]), add(a[half:], b[half:])) for a, b in zip(keep, got))
    )
    return jnp.concatenate(keeps, axis=2), jnp.concatenate(sends, axis=2)


def halve_both(clock, keep, got):
    *values, = clock.tie(*keep, *got)
    half = keep[0].shape[0] // 2
    sums = [add(a, b) for a, b in zip(values[:2], values[2:])]
    send = jnp.concatenate([v[half:] for v in sums], axis=1)
    clock.mark = send
    return jnp.concatenate([v[:half] for v in sums], axis=1), send


def whole_sum(clock, moves, keep, got):
    keep, got = clock.tie(keep, got)
    held = sum_rest(moves, add(keep, got))
    clock.mark = held
    return held


def join(clock, *parts):
    parts = clock.tie(*parts)
    held = jnp.concatenate(parts, axis=0)
    clock.mark = held
    return held


def split(clock, *parts):
    parts = clock.tie(*parts)
    held = jnp.concatenate(parts, axis=0)
    half = held.shape[1] // 2
    first, second = held[:, :half], held[:, half:]
    clock.mark = second
    return first, second


def on_device(
    moves,
    tokens,
    seg_starts,
    w_qkv,
    b_query,
    b_value,
    w_out,
    b_out,
    gain_one,
    beta_one,
    w_up,
    b_up,
    w_down,
    b_down,
    gain_two,
    beta_two,
    cotangent,
):
    rows, group, width = tokens.shape
    hidden = w_up.shape[1]
    quad, core, z = lax.axis_index("quad"), lax.axis_index("core"), lax.axis_index("seq")
    odd = z & 1
    x_bit, y_bit = quad & 1, quad >> 1
    z_bits = (z & 1) * 2 + (z >> 1)
    x_first = core * 16 + x_bit * 8 + y_bit * 4 + z_bits
    y_first = core * 16 + y_bit * 8 + x_bit * 4 + z_bits
    ids = jnp.stack([x_first, y_first, x_first, y_first]).astype(jnp.int32)
    line = lambda vector: vector.reshape(1, -1)

    def to_rows(values):
        return [
            lax.ppermute(jnp.where(odd == k, values[0], values[1]), LINE, moves.to_rows[k])
            for k in range(2)
        ]

    def from_rows(values):
        return [lax.ppermute(values[k], LINE, moves.from_rows[k]) for k in range(2)]

    def in_order(both):
        return jnp.where(odd == 0, jnp.stack(both), jnp.stack(both[::-1]))

    starts_here = jnp.where(odd == 0, seg_starts[0], seg_starts[1])
    starts_there = moves.core(starts_here)
    starts = jnp.where(core == z // 2, starts_here, starts_there)
    mine = to_rows(tokens)
    other = [moves.core(piece) for piece in mine]
    x_all = jnp.concatenate(mine + other, axis=0)
    count = 2 * group
    cotangent, x_all = lax.optimization_barrier((cotangent, x_all))
    cot = to_rows(cotangent)

    lane = jnp.arange(group, dtype=jnp.int32)
    positions = jnp.concatenate(
        [(2 * side + (odd ^ k)) * group + lane for side in (core, 1 - core) for k in range(2)]
    )
    seg = jnp.sum((starts[None, :] <= positions[:, None]).astype(jnp.int32), axis=1)
    same = seg[:, None] == jnp.arange(128, dtype=jnp.int32)[None, :]
    qhot = same[:count].astype(BF16)
    khot = jnp.where(same, 0.0, NEGATIVE).astype(BF16)

    q, k, v, attn, lse = attend(x_all, w_qkv, line(b_query), line(b_value), qhot, khot)
    mixed0, mixed1, n1, unit, inv, slope, dh2, dffn, vec_two, d_send, d_keep = forward(
        ids, x_all, attn, w_out, line(b_out), line(gain_one), line(beta_one), w_up, line(b_up), w_down,
        line(b_down), line(gain_two), line(beta_two), cot,
    )
    clock = Clock()
    clock.mark = dffn
    core_swap, quad_swap, line_swap = moves.core, moves.quad, moves.line
    d_got = core_swap(d_send)
    u_send, bu_there, part = back(4, ids, dffn, w_down, w_up, slope, n1, dh2)
    clock.mark = part
    u_got = core_swap(u_send)
    d_sums, d_send = send_blocks(clock, [d_keep, d_got], 8, 16)
    d_sums.append(quad_swap(d_send, 1))
    mixed = from_rows(clock.tie(mixed0, mixed1))
    (dffn,) = clock.tie(dffn)
    u_keep, bu_here, dh1, dattn, o_send, o_keep, vec_one = back(
        0, ids, dffn, w_down, w_up, slope, n1, part, unit, inv, line(gain_one), attn, w_out
    )
    clock.mark = vec_one
    u_keep, *mixed = clock.tie(u_keep, *mixed)
    u_sums, u_send = send_blocks(clock, [u_keep, u_got], 8, 16)
    u_sums.append(quad_swap(u_send, 2))
    heads = (ids, x_all, q, k, v)
    tail = (attn, lse, qhot, khot)
    (dattn,) = clock.tie(dattn)
    a_send, a_keep, *grads_a, vec_a = attend_back(0, *heads, dattn, *tail)
    clock.mark = vec_a
    a_got = core_swap(a_send)
    d_sums, d_send = send_blocks(clock, d_sums, 4, 8)
    d_sums.append(quad_swap(d_send, 2))
    (dattn,) = clock.tie(dattn)
    b_send, b_keep, *grads_b, vec_b = attend_back(1, *heads, dattn, *tail)
    clock.mark = vec_b
    b_got = core_swap(b_send)
    u_sums, u_send = send_blocks(clock, u_sums, 4, 8)
    u_sums.append(quad_swap(u_send, 1))
    (dattn,) = clock.tie(dattn)
    c_send, c_keep, *grads_c, vec_c = attend_back(2, *heads, dattn, *tail)
    clock.mark = vec_c
    c_got = core_swap(c_send)
    o_got = core_swap(clock.tie(o_send)[0])

    def close(*values):
        return lax.optimization_barrier(values)

    du_keep, du_send = halve_parts(clock, d_sums, u_sums)
    du_got = line_swap(du_send, 1)
    bu_here, bu_there, vec_one, vec_two, vec_a, vec_b, vec_c, _ = close(
        bu_here, bu_there, vec_one, vec_two, vec_a, vec_b, vec_c, du_send
    )
    bu_here, bu_there = bu_here[:, 0].reshape(1, -1), bu_there[:, 0].reshape(1, -1)
    g_bu = jnp.where(
        core == 0,
        jnp.concatenate([bu_here, bu_there], axis=1),
        jnp.concatenate([bu_there, bu_here], axis=1),
    )
    vec_zero = jnp.concatenate([vec_a, vec_b, vec_c], axis=1)
    vectors = jnp.concatenate(
        [vec_zero[:2], vec_one[:3], vec_two[:3], g_bu.reshape(-1, width)], axis=0
    )
    vec_got = core_swap(vectors)
    a_keep, a_got, b_keep, b_got, vectors, vec_got = close(
        (a_keep, o_keep), (a_got, o_got), (b_keep, c_keep), (b_got, c_got), vectors, vec_got
    )
    clock.stop()
    a_keep, a_send = halve_wide(a_keep, a_got)
    b_keep, b_send = halve_wide(b_keep, b_got)
    a_got, b_got = quad_swap(a_send, 1), quad_swap(b_send, 2)
    vectors = vectors + vec_got
    vec_got = quad_swap(vectors, 1)
    du_keep, du_got, _, _ = close(du_keep, du_got, a_send, b_send)
    du_keep, du_send = halve(clock, du_keep, du_got)
    du_got = line_swap(du_send, 2)
    dh1, _ = close(dh1, du_send)
    dx, there = tokens_back(*zip(grads_a, grads_b, grads_c), w_qkv, dh1)
    du_keep, du_got, a_keep, a_got, b_keep, b_got, there, vectors, vec_got = close(
        du_keep, du_got, a_keep, a_got, b_keep, b_got, there, vectors, vec_got
    )
    du = whole_sum(clock, moves, du_keep, du_got)
    du_got = line_swap(du, 2)
    a_keep, a_send = halve(clock, a_keep, a_got)
    a_got = quad_swap(a_send, 2)
    b_keep, b_send = halve(clock, b_keep, b_got)
    b_got = quad_swap(b_send, 1)
    there_got = core_swap(there)
    vectors = vectors + vec_got
    vec_got = quad_swap(vectors, 2)
    du, du_got, a_keep, a_got, b_keep, b_got, there_got, vectors, vec_got = close(
        du, du_got, a_keep, a_got, b_keep, b_got, there_got, vectors, vec_got
    )
    du = join(clock, du, du_got)
    du_got = line_swap(du, 1)
    dx, there_got, _ = close(dx, there_got, du)
    dx = (dx + there_got.astype(F32)).astype(BF16)
    dx = (dx[:group], dx[group:])
    pick = (starts[:, None] == positions[None, :count]).astype(BF16)
    cls = dot(pick, jnp.concatenate(close(mixed0, mixed1, du)[:2], axis=0)).astype(BF16)
    cls = cls + core_swap(cls)
    cls = jnp.swapaxes(cls.reshape(cls.shape[0], moves.seq_count, -1), 0, 1)
    ab_keep, ab_send = halve_both(clock, (a_keep, b_keep), (a_got, b_got))
    vectors = sum_rest(moves, vectors + vec_got)
    vec_got = line_swap(vectors, 1)
    du, du_got, ab_send, ab_keep, *dx, cls, vectors, vec_got = close(
        du, du_got, ab_send, ab_keep, *dx, cls, vectors, vec_got
    )
    d, u = split(clock, du, du_got)
    d_got, u_got = quad_swap(d, 2), quad_swap(u, 1)
    ab_got = line_swap(ab_send, 1)
    vectors = vectors + vec_got
    vec_got = line_swap(vectors, 2)
    cls = [
        lax.ppermute(
            lax.dynamic_index_in_dim(cls, 2 * core + (m ^ odd), 0, keepdims=False), LINE, moves.to_rows[m]
        )
        for m in range(2)
    ]
    d, d_got, u, u_got, ab_keep, ab_got, vectors, vec_got, *cls = close(
        d, d_got, u, u_got, ab_keep, ab_got, vectors, vec_got, *cls
    )
    d = join(clock, d, d_got)
    u = join(clock, u, u_got)
    d_got, u_got = quad_swap(d, 1), quad_swap(u, 2)
    ab_keep, ab_got, _, _ = close(ab_keep, ab_got, d, u)
    ab_keep, ab_send = halve(clock, ab_keep, ab_got)
    ab_got = line_swap(ab_send, 2)
    ab = whole_sum(clock, moves, ab_keep, ab_got)
    ab_got = line_swap(ab, 2)
    ab = join(clock, ab, ab_got)
    ab_got = line_swap(ab, 1)
    a, b = split(clock, ab, ab_got)
    a_got, b_got = quad_swap(a, 2), quad_swap(b, 1)
    d, d_got, u, u_got, *dx, vectors, vec_got, _, _ = close(
        d, d_got, u, u_got, *dx, vectors, vec_got, a, b
    )
    vectors = vectors + vec_got
    d = join(clock, d, d_got)
    u = join(clock, u, u_got)
    d_got, u_got = core_swap(d), core_swap(u)
    grad_tokens = from_rows(dx)
    a, a_got, b, b_got, d, u, vectors, grad_tokens[0] = close(
        a, a_got, b, b_got, d, u, vectors, grad_tokens[0]
    )
    a = join(clock, a, a_got)
    b = join(clock, b, b_got)
    a_got, b_got = quad_swap(a, 1), quad_swap(b, 2)
    d_got, u_got, _, _ = close(d_got, u_got, a, b)
    grad_w_down = unfold_down(ids, d, d_got, (hidden, width))
    grad_w_up = unfold_up(ids, u, u_got, (width, hidden))
    a, a_got, b, b_got, grad_w_down, grad_w_up, grad_tokens[1] = close(
        a, a_got, b, b_got, grad_w_down, grad_w_up, grad_tokens[1]
    )
    a = join(clock, a, a_got)
    b = join(clock, b, b_got)
    a_got, b_got = core_swap(a), core_swap(b)
    cls, grad_tokens, mixed = in_order(cls), in_order(grad_tokens), in_order(mixed)
    grad_w_qkv, grad_w_out = unfold_two(ids, a, a_got, b, b_got)
    return (
        mixed,
        cls,
        grad_tokens,
        grad_w_qkv,
        vectors[0],
        vectors[1],
        grad_w_out,
        vectors[4],
        vectors[2],
        vectors[3],
        grad_w_up,
        vectors[8:].reshape(-1),
        grad_w_down,
        vectors[7],
        vectors[5],
        vectors[6],
    )


def solution(mesh):
    pairs, seq_count = mesh.shape["dp"] // 2, mesh.shape["seq"]
    axes = ("rest", "quad", "core", "seq")
    split = jax.sharding.Mesh(mesh.devices.reshape(pairs // 4, 4, 2, seq_count), axes)
    dp = ("rest", "quad", "core")
    row = P(dp, "seq", None)
    in_specs = (row, P(dp, None)) + (P(),) * 13 + (row,)
    out_specs = (row, P(dp, None, "seq"), row) + (P(),) * 13
    return jax.shard_map(
        partial(on_device, Moves(pairs, seq_count)),
        mesh=split,
        in_specs=in_specs,
        out_specs=out_specs,
        check_vma=False,
    )
```

time: 1470 us -> 333 us (0.23); the launches traced: 1450 us -> 326 us
  blocking collectives: 458 us -> 0 us
  local copies, waits for them, and re-layouts: 383 us -> 13.1 us
  waiting for transfers between devices: 364 us -> 77.3 us
  matrix products: 176 us -> 0.25 us
  Pallas kernels: 0 us -> 138 us
  starting transfers between devices: 1.04 us -> 67 us
  other arithmetic: 48.3 us -> 29.1 us
    unnamed x1 -> x0, blocking collectives: 458 us -> none
    unnamed x8 -> x0, waiting for transfers between devices: 240 us -> none
    unnamed x130 -> x82, local copies, waits for them, and re-layouts: 232 us -> 3.68 us
    dot_general x35 -> x1, matrix products: 176 us -> 0.25 us  [dot(): return lax.dot_general(a, b, dims, preferred_element_type=F32)]
    pallas_call x0 -> x11, Pallas kernels: none -> 138 us  [the longest x3 47.7 us: attend_back(): call(partial(attend_back_body, quad), (1,), [whole(x_all.shape), column(c...]
    all_gather x2 -> x0, waiting for transfers between devices: 88.5 us -> none  [the longest x1 57.7 us: on_device(): add_key_piece = lax.all_gather(key_b, 'seq', axis=1, tiled=True)]
    ppermute x0 -> x54, waiting for transfers between devices: none -> 77.3 us  [the longest x44 69.7 us: swap(): return lax.ppermute(values, axis, [(i, i ^ bit) for i in range(count)])]
    ppermute x0 -> x54, starting transfers between devices: none -> 67 us  [the longest x44 55 us: swap(): return lax.ppermute(values, axis, [(i, i ^ bit) for i in range(count)])]
  transfers between devices with their start and end apart: 6 -> 54, of which waited for: 4 -> 18; matrix products, arithmetic and copies ran while one was open for 26% -> 11% of each run, Pallas kernels for 0% -> 33%
where the time goes in v1:
time: 333 us; the launch traced here: 326 us
  Pallas kernels  138 us (41%)
  waiting for transfers between devices  77.3 us (23%)
  starting transfers between devices  67 us (20%)
  other arithmetic  29.1 us (9%)
  local copies, waits for them, and re-layouts  13.1 us (4%)
    ppermute x44, waiting for transfers between devices, swap(): return lax.ppermute(values, axis, [(i, i ^ bit) for i in range(count)])  69.7 us
    ppermute x44, starting transfers between devices, swap(): return lax.ppermute(values, axis, [(i, i ^ bit) for i in range(count)])  55 us
    pallas_call x3, Pallas kernels, attend_back(): call(partial(attend_back_body, quad), (1,), [whole(x_all.shape), column(c...  47.7 us
    pallas_call x2, Pallas kernels, back(): call(body, (4,), in_specs, out_specs, out_shape, scratch, 5000000000, 160...  25.6 us
    pallas_call x1, Pallas kernels, forward(): call(forward_body, (UP_STEPS + CHUNKS,), [whole((count, width)), whole((c...  23.8 us
    pallas_call x1, Pallas kernels, attend(): call(attend_body, (quads,), [whole(x_all.shape), *weight, column(1), colu...  15.7 us
    convert_element_type x6, other arithmetic, total(): return sum((part.astype(F32) for part in parts)).astype(BF16)  11.6 us
    ppermute x4, starting transfers between devices, to_rows(): lax.ppermute(jnp.where(odd == k, values[0], values[1]), LINE, moves.to_ro...  8.85 us
  transfers between devices with their start and end apart: 54, of which 18 were waited for; matrix products, arithmetic and copies ran while one was open for 11% of the time, Pallas kernels for 33%

profile of v1, /device:TPU:0, one launch (start us, length us, event | category | flops | bytes accessed | tf_op | source)
XLA Modules:
  0.0 326.2 jit_solution(11712476366719434628)
XLA Ops:
  3.8 2.6 collective-permute-start.1
  12.1 10.6 %collective-permute-start.2 = (bf16[256,768]{1,0:T(8,128)(2,1)S(1)}, bf16[256,768]{1,0:T(8,128)(2,1)S(1)}, u32[]{:S(2)}, u32[]{:S(2)}) collective-permute-start(bf16[256,768]{1,0:T(8,128)(2,1)S(1)} %collective-permute-done), channel_id=1, source_target_pairs={{0,4},{4,0},{1,5},{5,1},{2,6},{6,2},{3,7},{7,3},{8,12},{12,8},{9,1... | collective-permute-start | bytes 1179656 | tf_op jit(solution)/shard_map/ppermute | solution.py:576
  25.9 4.8 %collective-permute-start.6 = (bf16[256,768]{1,0:T(8,128)(2,1)S(1)}, bf16[256,768]{1,0:T(8,128)(2,1)S(1)}, u32[]{:S(2)}, u32[]{:S(2)}) collective-permute-start(bf16[256,768]{1,0:T(8,128)(2,1)S(1)} %get-tuple-element.378), channel_id=1, source_target_pairs={{0,1},{1,0},{2,5},{3,4},{4,3},{5,2},{6,7},{7,6},{8,9},{9,8},{10,13... | collective-permute-start | bytes 1179656 | tf_op jit(solution)/shard_map/ppermute | solution.py:712
  31.4 15.7 %shard_map.279 = (bf16[512,768]{1,0:T(8,128)(2,1)}, bf16[1024,768]{1,0:T(8,128)(2,1)}, bf16[1024,768]{1,0:T(8,128)(2,1)}, f32[512,768]{1,0:T(8,128)}, f32[3,8,512]{2,1,0:T(8,128)}) custom-call(bf16[1024,768]{1,0:T(8,128)(2,1)} %pad_maximum_fusion.x_ref, bf16[768,2304]{1,0:T(8,128)(2,1)} %refs_9_.1, bf16[768,2304]{1,0:T(8,128)(2,1)} %refs_9_.1, ...), custom_call_target="tpu_custom_call" | custom-call | flops 12999999488 | bytes 16000000 | tf_op jit(solution)/shard_map/pallas_call | solution.py:91
  48.0 23.8 %shard_map.280 = (bf16[256,768]{1,0:T(8,128)(2,1)}, bf16[256,768]{1,0:T(8,128)(2,1)}, bf16[512,768]{1,0:T(8,128)(2,1)}, f32[512,768]{1,0:T(8,128)}, f32[512,128]...) custom-call(s32[4]{0:T(128)} %pad_add_fusion.2.ids, ...), custom_call_target="tpu_custom_call" | custom-call | flops 8000000000 | bytes 30000000 | tf_op jit(solution)/shard_map/pallas_call | solution.py:211
  71.9 3.2 collective-permute-start.7
  75.1 10.5 %shard_map.281 = (bf16[16,96,768]{2,1,0:T(8,128)(2,1)}, f32[4,8,384]{2,1,0:T(8,128)}, f32[512,768]{1,0:T(8,128)}) custom-call(s32[4]{0:T(128)} %pad_add_fusion.2.ids, bf16[512,768]{1,0:T(8,128)(2,1)} %get-tuple-element.194.dffn_ref, bf16[3072,768]{1,0:T(8,128)(2,1)} %wd_ref.5, bf16[768,3072]{1,0:T(8,128)(2,1)} %wu_ref.5, ...), custom_call_target="tpu_custom_call" | custom-call | flops 5000000000 | bytes 16000000 | tf_op jit(solution)/shard_map/pallas_call | solution.py:340
  90.4 15.2 %shard_map.282 = (bf16[16,96,768]{2,1,0:T(8,128)(2,1)}, f32[4,8,384]{2,1,0:T(8,128)}, f32[512,768]{1,0:T(8,128)}, bf16[512,768]{1,0:T(8,128)(2,1)}, bf16[16,48,3...) custom-call(s32[4]{0:T(128)} %pad_add_fusion.2.ids, ...), custom_call_target="tpu_custom_call" | custom-call | flops 5000000000 | bytes 16000000 | tf_op jit(solution)/shard_map/pallas_call | solution.py:340
  109.4 12.5 %shard_map.283 = (bf16[16,48,384]{2,1,0:T(8,128)(2,1)}, bf16[16,48,384]{2,1,0:T(8,128)(2,1)}, bf16[512,256]{1,0:T(8,128)(2,1)}, bf16[1024,256]{1,0:T(8,128)(2,1)...) custom-call(s32[4]{0:T(128)} %pad_add_fusion.2.ids, bf16[1024,768]{1,0:T(8,128)(2,1)} %pad_maximum_fusion.x_ref, ...), custom_call_target="tpu_custom_call" | custom-call | flops 12000000000 | bytes 10000000 | tf_op jit(solution)/shard_map/pallas_call | solution.py:396
  121.9 3.5 %collective-permute-start.16 = (bf16[16,48,384]{2,1,0:T(8,128)(2,1)}, bf16[16,48,384]{2,1,0:T(8,128)(2,1)}, u32[]{:S(2)}, u32[]{:S(2)}) collective-permute-start(bf16[16,48,384]{2,1,0:T(8,128)(2,1)} %get-tuple-element.236), channel_id=1, source_target_pairs={{0,4},{4,0},{1,5},{5,1},{2,6},{6,2},{3,7},{7,3},{8,12},{12,8},{9,1... | collective-permute-start | bytes 1769480 | tf_op jit(solution)/shard_map/ppermute | solution.py:576
  129.0 12.7 %shard_map.284 = (bf16[16,48,384]{2,1,0:T(8,128)(2,1)}, bf16[16,48,384]{2,1,0:T(8,128)(2,1)}, bf16[512,256]{1,0:T(8,128)(2,1)}, bf16[1024,256]{1,0:T(8,128)(2,1)...) custom-call(s32[4]{0:T(128)} %pad_add_fusion.2.ids, bf16[1024,768]{1,0:T(8,128)(2,1)} %pad_maximum_fusion.x_ref, ...), custom_call_target="tpu_custom_call" | custom-call | flops 12000000000 | bytes 10000000 | tf_op jit(solution)/shard_map/pallas_call | solution.py:396
  141.7 2.3 add_convert_fusion.3
  144.5 22.6 %shard_map.285 = (bf16[16,48,384]{2,1,0:T(8,128)(2,1)}, bf16[16,48,384]{2,1,0:T(8,128)(2,1)}, bf16[512,256]{1,0:T(8,128)(2,1)}, bf16[1024,256]{1,0:T(8,128)(2,1)...) custom-call(s32[4]{0:T(128)} %pad_add_fusion.2.ids, bf16[1024,768]{1,0:T(8,128)(2,1)} %pad_maximum_fusion.x_ref, ...), custom_call_target="tpu_custom_call" | custom-call | flops 12000000000 | bytes 10000000 | tf_op jit(solution)/shard_map/pallas_call | solution.py:396
  173.3 3.1 collective-permute-start.15
  184.1 6.1 %collective-permute-done.15 = bf16[2,192,768]{2,1,0:T(8,128)(2,1)S(1)} collective-permute-done((bf16[2,192,768]{2,1,0:T(8,128)(2,1)S(1)}, bf16[2,192,768]{2,1,0:T(8,128)(2,1)S(1)}, u32[]{:S(2)}, u32[]{:S(2)}) %collective-permute-start.15) | collective-permute-done | bytes 589856 | tf_op jit(solution)/shard_map/ppermute | solution.py:576
  190.3 2.5 collective-permute-start.21
  192.7 8.3 %shard_map.286 = (f32[512,768]{1,0:T(8,128)}, bf16[512,768]{1,0:T(8,128)(2,1)}) custom-call(bf16[512,256]{1,0:T(8,128)(2,1)} %get-tuple-element.263.refs_0_, bf16[512,256]{1,0:T(8,128)(2,1)} %get-tuple-element.264.refs_1_, bf16[512,256]{1,0:T(8,128)(2,1)} %get-tuple-element.265.refs_2_, bf16[1024,256]{1,0:T(8,128)(2,1)} %get-tuple-element.266.refs_3_, ...), custom_call_target="tpu_custom_call" | custom-call | flops 6000000000 | bytes 12000000 | tf_op jit(solution)/shard_map/pallas_call | solution.py:437
  201.0 5.2 %collective-permute-done.21 = bf16[1,192,768]{2,1,0:T(8,128)(2,1)S(1)} collective-permute-done((bf16[1,192,768]{2,1,0:T(8,128)(2,1)S(1)}, bf16[1,192,768]{2,1,0:T(8,128)(2,1)S(1)}, u32[]{:S(2)}, u32[]{:S(2)}) %collective-permute-start.21) | collective-permute-done | bytes 294944 | tf_op jit(solution)/shard_map/ppermute | solution.py:576
  210.5 6.7 %collective-permute-done.29 = f32[12,768]{1,0:T(8,128)S(1)} collective-permute-done((f32[12,768]{1,0:T(8,128)S(1)}, f32[12,768]{1,0:T(8,128)S(1)}, u32[]{:S(2)}, u32[]{:S(2)}) %collective-permute-start.29) | collective-permute-done | bytes 36896 | tf_op jit(solution)/shard_map/ppermute | solution.py:576
  217.2 3.9 %collective-permute-done.25 = bf16[1,192,768]{2,1,0:T(8,128)(2,1)S(1)} collective-permute-done((bf16[1,192,768]{2,1,0:T(8,128)(2,1)S(1)}, bf16[1,192,768]{2,1,0:T(8,128)(2,1)S(1)}, u32[]{:S(2)}, u32[]{:S(2)}) %collective-permute-start.25) | collective-permute-done | bytes 294944 | tf_op jit(solution)/shard_map/ppermute | solution.py:576
  226.1 11.4 %collective-permute-done.32 = f32[12,768]{1,0:T(8,128)S(1)} collective-permute-done((f32[12,768]{1,0:T(8,128)S(1)}, f32[12,768]{1,0:T(8,128)S(1)}, u32[]{:S(2)}, u32[]{:S(2)}) %collective-permute-start.32) | collective-permute-done | bytes 36896 | tf_op jit(solution)/shard_map/ppermute | solution.py:576
  243.3 6.2 %collective-permute-done.38 = bf16[8,192]{1,0:T(8,128)(2,1)S(1)} collective-permute-done((bf16[8,192]{1,0:T(8,128)(2,1)S(1)}, bf16[8,192]{1,0:T(8,128)(2,1)S(1)}, u32[]{:S(2)}, u32[]{:S(2)}) %collective-permute-start.38) | collective-permute-done | bytes 3104 | tf_op jit(solution)/shard_map/ppermute | solution.py:853
  257.8 6.4 %collective-permute-done.39 = bf16[1,96,768]{2,1,0:T(8,128)(2,1)S(1)} collective-permute-done((bf16[1,96,768]{2,1,0:T(8,128)(2,1)S(1)}, bf16[1,96,768]{2,1,0:T(8,128)(2,1)S(1)}, u32[]{:S(2)}, u32[]{:S(2)}) %collective-permute-start.39) | collective-permute-done | bytes 147488 | tf_op jit(solution)/shard_map/ppermute | solution.py:576
  265.3 8.3 %collective-permute-done.40 = bf16[1,96,768]{2,1,0:T(8,128)(2,1)S(1)} collective-permute-done((bf16[1,96,768]{2,1,0:T(8,128)(2,1)S(1)}, bf16[1,96,768]{2,1,0:T(8,128)(2,1)S(1)}, u32[]{:S(2)}, u32[]{:S(2)}) %collective-permute-start.40) | collective-permute-done | bytes 147488 | tf_op jit(solution)/shard_map/ppermute | solution.py:576
  273.7 8.2 %collective-permute-done.41 = bf16[2,96,768]{2,1,0:T(8,128)(2,1)S(1)} collective-permute-done((bf16[2,96,768]{2,1,0:T(8,128)(2,1)S(1)}, bf16[2,96,768]{2,1,0:T(8,128)(2,1)S(1)}, u32[]{:S(2)}, u32[]{:S(2)}) %collective-permute-start.41) | collective-permute-done | bytes 294944 | tf_op jit(solution)/shard_map/ppermute | solution.py:576
  282.0 2.7 collective-permute-done.45
  288.7 5.0 %collective-permute-done.43 = bf16[4,48,768]{2,1,0:T(8,128)(2,1)S(1)} collective-permute-done((bf16[4,48,768]{2,1,0:T(8,128)(2,1)S(1)}, bf16[4,48,768]{2,1,0:T(8,128)(2,1)S(1)}, u32[]{:S(2)}, u32[]{:S(2)}) %collective-permute-start.43) | collective-permute-done | bytes 294944 | tf_op jit(solution)/shard_map/ppermute | solution.py:576
  294.5 2.5 collective-permute-start.48
  298.7 5.3 %shard_map.287 = f32[3072,768]{1,0:T(8,128)} custom-call(s32[4]{0:T(128)S(1)} %copy-done, bf16[16,96,768]{2,1,0:T(8,128)(2,1)S(1)} %constant_dynamic-update-slice_fusion.8.own_ref, bf16[16,96,768]{2,1,0:T(8,128)(2,1)S(1)} %collective-permute-done.49.other_ref), custom_call_target="tpu_custom_call" | custom-call | bytes 16000000 | tf_op jit(solution)/shard_map/pallas_call | solution.py:464
  304.1 5.3 %shard_map.288 = f32[768,3072]{1,0:T(8,128)} custom-call(s32[4]{0:T(128)S(1)} %copy-done, bf16[16,96,768]{2,1,0:T(8,128)(2,1)S(1)} %constant_dynamic-update-slice_fusion.10.own_ref, bf16[16,96,768]{2,1,0:T(8,128)(2,1)S(1)} %collective-permute-done.50.other_ref), custom_call_target="tpu_custom_call" | custom-call | bytes 16000000 | tf_op jit(solution)/shard_map/pallas_call | solution.py:498
  317.9 2.4 maximum_select_fusion.1
  320.3 5.8 %shard_map.289 = (f32[768,2304]{1,0:T(8,128)}, f32[768,768]{1,0:T(8,128)}) custom-call(s32[4]{0:T(128)S(1)} %copy-done, bf16[16,48,768]{2,1,0:T(8,128)(2,1)S(1)} %constant_dynamic-update-slice_fusion.16.a_own, bf16[16,48,768]{2,1,0:T(8,128)(2,1)} %collective-permute-done.52.a_other, bf16[16,48,768]{2,1,0:T(8,128)(2,1)S(1)} %constant_dynamic-update-slice_fusion.18.b_own, ...), custom_call_target="tpu_custom_call" | custom-call | bytes 16000000 | tf_op jit(solution)/shard_map/pallas_call | solution.py:542
  (258 shorter events, 79.1 us)
Async XLA Ops:
  3.8 18.8 %collective-permute-start.1 = (bf16[256,768]{1,0:T(8,128)(2,1)S(1)}, bf16[256,768]{1,0:T(8,128)(2,1)S(1)}, u32[]{:S(2)}, u32[]{:S(2)}) collective-permute-start(bf16[256,768]{1,0:T(8,128)(2,1)S(1)} %get-tuple-element.381), channel_id=1, source_target_pairs={{0,1},{1,0},{2,5},{3,4},{4,3},{5,2},{6,7},{7,6},{8,9},{9,8},{10,13... | collective-permute-start | bytes 1179656 | tf_op jit(solution)/shard_map/ppermute | solution.py:712
  25.9 21.3 %collective-permute-start.6 = (bf16[256,768]{1,0:T(8,128)(2,1)S(1)}, bf16[256,768]{1,0:T(8,128)(2,1)S(1)}, u32[]{:S(2)}, u32[]{:S(2)}) collective-permute-start(bf16[256,768]{1,0:T(8,128)(2,1)S(1)} %get-tuple-element.378), channel_id=1, source_target_pairs={{0,1},{1,0},{2,5},{3,4},{4,3},{5,2},{6,7},{7,6},{8,9},{9,8},{10,13... | collective-permute-start | bytes 1179656 | tf_op jit(solution)/shard_map/ppermute | solution.py:712
  30.8 16.4 %collective-permute-start.5 = (bf16[256,768]{1,0:T(8,128)(2,1)S(1)}, bf16[256,768]{1,0:T(8,128)(2,1)S(1)}, u32[]{:S(2)}, u32[]{:S(2)}) collective-permute-start(bf16[256,768]{1,0:T(8,128)(2,1)S(1)} %get-tuple-element.379), channel_id=1, source_target_pairs={{0,0},{1,1},{2,4},{3,5},{4,2},{5,3},{6,6},{7,7},{8,8},{9,9},{10,12... | collective-permute-start | bytes 1179656 | tf_op jit(solution)/shard_map/ppermute | solution.py:712
  71.9 13.7 %collective-permute-start.7 = (bf16[16,96,768]{2,1,0:T(8,128)(2,1)}, bf16[16,96,768]{2,1,0:T(8,128)(2,1)}, u32[]{:S(2)}, u32[]{:S(2)}) collective-permute-start(bf16[16,96,768]{2,1,0:T(8,128)(2,1)} %get-tuple-element.187), channel_id=1, source_target_pairs={{0,4},{4,0},{1,5},{5,1},{2,6},{6,2},{3,7},{7,3},{8,12},{12,8},{9,1... | collective-permute-start | bytes 7077896 | tf_op jit(solution)/shard_map/ppermute | solution.py:576
  85.5 20.0 %collective-permute-start.11 = (bf16[16,96,768]{2,1,0:T(8,128)(2,1)}, bf16[16,96,768]{2,1,0:T(8,128)(2,1)}, u32[]{:S(2)}, u32[]{:S(2)}) collective-permute-start(bf16[16,96,768]{2,1,0:T(8,128)(2,1)} %get-tuple-element.210), channel_id=1, source_target_pairs={{0,4},{4,0},{1,5},{5,1},{2,6},{6,2},{3,7},{7,3},{8,12},{12,8},{9,1... | collective-permute-start | bytes 7077896 | tf_op jit(solution)/shard_map/ppermute | solution.py:576
  87.2 38.1 %collective-permute-start.10 = (bf16[8,96,768]{2,1,0:T(8,128)(2,1)S(1)}, bf16[8,96,768]{2,1,0:T(8,128)(2,1)S(1)}, u32[]{:S(2)}, u32[]{:S(2)}) collective-permute-start(bf16[8,96,768]{2,1,0:T(8,128)(2,1)S(1)} %add_convert_fusion.1), channel_id=1, source_target_pairs={{0,8},{8,0},{16,24},{24,16},{1,9},{9,1},{17,25},{25,17},{2,10},{10... | collective-permute-start | bytes 3538952 | tf_op jit(solution)/shard_map/ppermute | solution.py:576
  88.8 16.8 %collective-permute-start.8 = (bf16[256,768]{1,0:T(8,128)(2,1)S(1)}, bf16[256,768]{1,0:T(8,128)(2,1)S(1)}, u32[]{:S(2)}, u32[]{:S(2)}) collective-permute-start(bf16[256,768]{1,0:T(8,128)(2,1)S(1)} %copy-done.30), channel_id=1, source_target_pairs={{0,0},{1,1},{4,2},{5,3},{2,4},{3,5},{6,6},{7,7},{8,8},{9,9},{12,10... | collective-permute-start | bytes 1179656 | tf_op jit(solution)/shard_map/ppermute | solution.py:717
  89.7 15.8 %collective-permute-start.9 = (bf16[256,768]{1,0:T(8,128)(2,1)S(1)}, bf16[256,768]{1,0:T(8,128)(2,1)S(1)}, u32[]{:S(2)}, u32[]{:S(2)}) collective-permute-start(bf16[256,768]{1,0:T(8,128)(2,1)S(1)} %copy-done.32), channel_id=1, source_target_pairs={{1,0},{0,1},{5,2},{4,3},{3,4},{2,5},{7,6},{6,7},{9,8},{8,9},{13,10... | collective-permute-start | bytes 1179656 | tf_op jit(solution)/shard_map/ppermute | solution.py:717
  107.8 33.9 %collective-permute-start.13 = (bf16[8,96,768]{2,1,0:T(8,128)(2,1)S(1)}, bf16[8,96,768]{2,1,0:T(8,128)(2,1)}, u32[]{:S(2)}, u32[]{:S(2)}) collective-permute-start(bf16[8,96,768]{2,1,0:T(8,128)(2,1)S(1)} %add_convert_fusion), channel_id=1, source_target_pairs={{0,16},{8,24},{16,0},{24,8},{1,17},{9,25},{17,1},{25,9},{2,18},{10... | collective-permute-start | bytes 3538952 | tf_op jit(solution)/shard_map/ppermute | solution.py:576
  121.9 51.4 %collective-permute-start.16 = (bf16[16,48,384]{2,1,0:T(8,128)(2,1)}, bf16[16,48,384]{2,1,0:T(8,128)(2,1)}, u32[]{:S(2)}, u32[]{:S(2)}) collective-permute-start(bf16[16,48,384]{2,1,0:T(8,128)(2,1)} %get-tuple-element.236), channel_id=1, source_target_pairs={{0,4},{4,0},{1,5},{5,1},{2,6},{6,2},{3,7},{7,3},{8,12},{12,8},{9,1... | collective-permute-start | bytes 1769480 | tf_op jit(solution)/shard_map/ppermute | solution.py:576
  128.5 38.8 %collective-permute-start.12 = (bf16[4,96,768]{2,1,0:T(8,128)(2,1)}, bf16[4,96,768]{2,1,0:T(8,128)(2,1)}, u32[]{:S(2)}, u32[]{:S(2)}) collective-permute-start(bf16[4,96,768]{2,1,0:T(8,128)(2,1)} %add_convert_fusion.4), channel_id=1, source_target_pairs={{0,16},{8,24},{16,0},{24,8},{1,17},{9,25},{17,1},{25,9},{2,18},{10... | collective-permute-start | bytes 1769480 | tf_op jit(solution)/shard_map/ppermute | solution.py:576
  141.7 34.7 %collective-permute-start.18 = (bf16[16,48,384]{2,1,0:T(8,128)(2,1)}, bf16[16,48,384]{2,1,0:T(8,128)(2,1)}, u32[]{:S(2)}, u32[]{:S(2)}) collective-permute-start(bf16[16,48,384]{2,1,0:T(8,128)(2,1)} %get-tuple-element.241), channel_id=1, source_target_pairs={{0,4},{4,0},{1,5},{5,1},{2,6},{6,2},{3,7},{7,3},{8,12},{12,8},{9,1... | collective-permute-start | bytes 1769480 | tf_op jit(solution)/shard_map/ppermute | solution.py:576
  144.0 23.6 %collective-permute-start.14 = (bf16[4,96,768]{2,1,0:T(8,128)(2,1)}, bf16[4,96,768]{2,1,0:T(8,128)(2,1)}, u32[]{:S(2)}, u32[]{:S(2)}) collective-permute-start(bf16[4,96,768]{2,1,0:T(8,128)(2,1)} %add_convert_fusion.3), channel_id=1, source_target_pairs={{0,8},{8,0},{16,24},{24,16},{1,9},{9,1},{17,25},{25,17},{2,10},{10... | collective-permute-start | bytes 1769480 | tf_op jit(solution)/shard_map/ppermute | solution.py:576
  173.3 16.8 %collective-permute-start.15 = (bf16[2,192,768]{2,1,0:T(8,128)(2,1)S(1)}, bf16[2,192,768]{2,1,0:T(8,128)(2,1)S(1)}, u32[]{:S(2)}, u32[]{:S(2)}) collective-permute-start(bf16[2,192,768]{2,1,0:T(8,128)(2,1)S(1)} %pad_maximum_fusion.2), channel_id=1, source_target_pairs={{0,1},{1,0},{2,3},{3,2},{4,5},{5,4},{6,7},{7,6},{8,9},{9,8},{10,11... | collective-permute-start | bytes 1769480 | tf_op jit(solution)/shard_map/ppermute | solution.py:576
  176.4 24.6 %collective-permute-start.24 = (f32[12,768]{1,0:T(8,128)S(1)}, f32[12,768]{1,0:T(8,128)S(1)}, u32[]{:S(2)}, u32[]{:S(2)}) collective-permute-start(f32[12,768]{1,0:T(8,128)S(1)} %add.249), channel_id=1, source_target_pairs={{0,8},{8,0},{16,24},{24,16},{1,9},{9,1},{17,25},{25,17},{2,10},{10... | collective-permute-start | bytes 110600 | tf_op jit(solution)/shard_map/ppermute | solution.py:576
  180.5 20.5 %collective-permute-start.23 = (bf16[8,48,768]{2,1,0:T(8,128)(2,1)S(1)}, bf16[8,48,768]{2,1,0:T(8,128)(2,1)S(1)}, u32[]{:S(2)}, u32[]{:S(2)}) collective-permute-start(bf16[8,48,768]{2,1,0:T(8,128)(2,1)S(1)} %pad_maximum_fusion.4), channel_id=1, source_target_pairs={{0,16},{8,24},{16,0},{24,8},{1,17},{9,25},{17,1},{25,9},{2,18},{10... | collective-permute-start | bytes 1769480 | tf_op jit(solution)/shard_map/ppermute | solution.py:576
  183.3 17.7 %collective-permute-start.22 = (bf16[8,48,768]{2,1,0:T(8,128)(2,1)S(1)}, bf16[8,48,768]{2,1,0:T(8,128)(2,1)S(1)}, u32[]{:S(2)}, u32[]{:S(2)}) collective-permute-start(bf16[8,48,768]{2,1,0:T(8,128)(2,1)S(1)} %pad_maximum_fusion.3), channel_id=1, source_target_pairs={{0,8},{8,0},{16,24},{24,16},{1,9},{9,1},{17,25},{25,17},{2,10},{10... | collective-permute-start | bytes 1769480 | tf_op jit(solution)/shard_map/ppermute | solution.py:576
  190.3 16.0 %collective-permute-start.21 = (bf16[1,192,768]{2,1,0:T(8,128)(2,1)S(1)}, bf16[1,192,768]{2,1,0:T(8,128)(2,1)S(1)}, u32[]{:S(2)}, u32[]{:S(2)}) collective-permute-start(bf16[1,192,768]{2,1,0:T(8,128)(2,1)S(1)} %get-tuple-element.374), channel_id=1, source_target_pairs={{0,2},{1,3},{2,0},{3,1},{4,6},{5,7},{6,4},{7,5},{8,10},{9,11},{10,... | collective-permute-start | bytes 884744 | tf_op jit(solution)/shard_map/ppermute | solution.py:576
  206.3 14.7 %collective-permute-start.25 = (bf16[1,192,768]{2,1,0:T(8,128)(2,1)S(1)}, bf16[1,192,768]{2,1,0:T(8,128)(2,1)S(1)}, u32[]{:S(2)}, u32[]{:S(2)}) collective-permute-start(bf16[1,192,768]{2,1,0:T(8,128)(2,1)S(1)} %add_convert_fusion.11), channel_id=1, source_target_pairs={{0,2},{1,3},{2,0},{3,1},{4,6},{5,7},{6,4},{7,5},{8,10},{9,11},{10,... | collective-permute-start | bytes 884744 | tf_op jit(solution)/shard_map/ppermute | solution.py:576
  206.4 14.7 %collective-permute-start.28 = (bf16[512,768]{1,0:T(8,128)(2,1)}, bf16[512,768]{1,0:T(8,128)(2,1)S(1)}, u32[]{:S(2)}, u32[]{:S(2)}) collective-permute-start(bf16[512,768]{1,0:T(8,128)(2,1)} %get-tuple-element.283), channel_id=1, source_target_pairs={{0,4},{4,0},{1,5},{5,1},{2,6},{6,2},{3,7},{7,3},{8,12},{12,8},{9,1... | collective-permute-start | bytes 2359304 | tf_op jit(solution)/shard_map/ppermute | solution.py:576
  206.6 14.4 %collective-permute-start.26 = (bf16[4,48,768]{2,1,0:T(8,128)(2,1)S(1)}, bf16[4,48,768]{2,1,0:T(8,128)(2,1)S(1)}, u32[]{:S(2)}, u32[]{:S(2)}) collective-permute-start(bf16[4,48,768]{2,1,0:T(8,128)(2,1)S(1)} %get-tuple-element.364), channel_id=1, source_target_pairs={{0,16},{8,24},{16,0},{24,8},{1,17},{9,25},{17,1},{25,9},{2,18},{10... | collective-permute-start | bytes 884744 | tf_op jit(solution)/shard_map/ppermute | solution.py:576
  208.3 12.8 %collective-permute-start.27 = (bf16[4,48,768]{2,1,0:T(8,128)(2,1)S(1)}, bf16[4,48,768]{2,1,0:T(8,128)(2,1)S(1)}, u32[]{:S(2)}, u32[]{:S(2)}) collective-permute-start(bf16[4,48,768]{2,1,0:T(8,128)(2,1)S(1)} %get-tuple-element.362), channel_id=1, source_target_pairs={{0,8},{8,0},{16,24},{24,16},{1,9},{9,1},{17,25},{25,17},{2,10},{10... | collective-permute-start | bytes 884744 | tf_op jit(solution)/shard_map/ppermute | solution.py:576
  221.1 16.4 %collective-permute-start.30 = (bf16[2,192,768]{2,1,0:T(8,128)(2,1)S(1)}, bf16[2,192,768]{2,1,0:T(8,128)(2,1)S(1)}, u32[]{:S(2)}, u32[]{:S(2)}) collective-permute-start(bf16[2,192,768]{2,1,0:T(8,128)(2,1)S(1)} %constant_dynamic-update-slice_fusion), channel_id=1, source_target_pairs={{0,1},{1,0},{2,3},{3,2},{4,5},{5,4},{6,7},{7,6},{8,9},{9,8},{10,11... | collective-permute-start | bytes 1769480 | tf_op jit(solution)/shard_map/ppermute | solution.py:576
  221.2 16.3 %collective-permute-start.32 = (f32[12,768]{1,0:T(8,128)S(1)}, f32[12,768]{1,0:T(8,128)S(1)}, u32[]{:S(2)}, u32[]{:S(2)}) collective-permute-start(f32[12,768]{1,0:T(8,128)S(1)} %add.260), channel_id=1, source_target_pairs={{0,1},{1,0},{2,3},{3,2},{4,5},{5,4},{6,7},{7,6},{8,9},{9,8},{10,11... | collective-permute-start | bytes 110600 | tf_op jit(solution)/shard_map/ppermute | solution.py:576
  237.7 14.5 %collective-permute-start.34 = (bf16[4,96,768]{2,1,0:T(8,128)(2,1)S(1)}, bf16[4,96,768]{2,1,0:T(8,128)(2,1)S(1)}, u32[]{:S(2)}, u32[]{:S(2)}) collective-permute-start(bf16[4,96,768]{2,1,0:T(8,128)(2,1)S(1)} %get-tuple-element.313), channel_id=1, source_target_pairs={{0,8},{8,0},{16,24},{24,16},{1,9},{9,1},{17,25},{25,17},{2,10},{10... | collective-permute-start | bytes 1769480 | tf_op jit(solution)/shard_map/ppermute | solution.py:576
  239.3 14.1 %collective-permute-start.33 = (bf16[4,96,768]{2,1,0:T(8,128)(2,1)S(1)}, bf16[4,96,768]{2,1,0:T(8,128)(2,1)S(1)}, u32[]{:S(2)}, u32[]{:S(2)}) collective-permute-start(bf16[4,96,768]{2,1,0:T(8,128)(2,1)S(1)} %get-tuple-element.311), channel_id=1, source_target_pairs={{0,16},{8,24},{16,0},{24,8},{1,17},{9,25},{17,1},{25,9},{2,18},{10... | collective-permute-start | bytes 1769480 | tf_op jit(solution)/shard_map/ppermute | solution.py:576
  256.7 28.0 %collective-permute-start.45 = (bf16[8,96,768]{2,1,0:T(8,128)(2,1)S(1)}, bf16[8,96,768]{2,1,0:T(8,128)(2,1)S(1)}, u32[]{:S(2)}, u32[]{:S(2)}) collective-permute-start(bf16[8,96,768]{2,1,0:T(8,128)(2,1)S(1)} %constant_dynamic-update-slice_fusion.6), channel_id=1, source_target_pairs={{0,16},{8,24},{16,0},{24,8},{1,17},{9,25},{17,1},{25,9},{2,18},{10... | collective-permute-start | bytes 3538952 | tf_op jit(solution)/shard_map/ppermute | solution.py:576
  257.4 27.7 %collective-permute-start.44 = (bf16[8,96,768]{2,1,0:T(8,128)(2,1)S(1)}, bf16[8,96,768]{2,1,0:T(8,128)(2,1)S(1)}, u32[]{:S(2)}, u32[]{:S(2)}) collective-permute-start(bf16[8,96,768]{2,1,0:T(8,128)(2,1)S(1)} %constant_dynamic-update-slice_fusion.4), channel_id=1, source_target_pairs={{0,8},{8,0},{16,24},{24,16},{1,9},{9,1},{17,25},{25,17},{2,10},{10... | collective-permute-start | bytes 3538952 | tf_op jit(solution)/shard_map/ppermute | solution.py:576
  285.4 13.4 %collective-permute-start.50 = (bf16[16,96,768]{2,1,0:T(8,128)(2,1)S(1)}, bf16[16,96,768]{2,1,0:T(8,128)(2,1)S(1)}, u32[]{:S(2)}, u32[]{:S(2)}) collective-permute-start(bf16[16,96,768]{2,1,0:T(8,128)(2,1)S(1)} %constant_dynamic-update-slice_fusion.10.own_ref), channel_id=1, source_target_pairs={{0,4},{4,0},{1,5},{5,1},{2,6},{6,2},{3,7},{7,3},{8,12},{12,8},{9,1... | collective-permute-start | bytes 7077896 | tf_op jit(solution)/shard_map/ppermute | solution.py:576
  285.5 13.2 %collective-permute-start.49 = (bf16[16,96,768]{2,1,0:T(8,128)(2,1)S(1)}, bf16[16,96,768]{2,1,0:T(8,128)(2,1)S(1)}, u32[]{:S(2)}, u32[]{:S(2)}) collective-permute-start(bf16[16,96,768]{2,1,0:T(8,128)(2,1)S(1)} %constant_dynamic-update-slice_fusion.8.own_ref), channel_id=1, source_target_pairs={{0,4},{4,0},{1,5},{5,1},{2,6},{6,2},{3,7},{7,3},{8,12},{12,8},{9,1... | collective-permute-start | bytes 7077896 | tf_op jit(solution)/shard_map/ppermute | solution.py:576
  294.5 16.3 %collective-permute-start.48 = (bf16[8,48,768]{2,1,0:T(8,128)(2,1)S(1)}, bf16[8,48,768]{2,1,0:T(8,128)(2,1)S(1)}, u32[]{:S(2)}, u32[]{:S(2)}) collective-permute-start(bf16[8,48,768]{2,1,0:T(8,128)(2,1)S(1)} %constant_dynamic-update-slice_fusion.14), channel_id=1, source_target_pairs={{0,16},{8,24},{16,0},{24,8},{1,17},{9,25},{17,1},{25,9},{2,18},{10... | collective-permute-start | bytes 1769480 | tf_op jit(solution)/shard_map/ppermute | solution.py:576
  297.1 14.8 %collective-permute-start.47 = (bf16[8,48,768]{2,1,0:T(8,128)(2,1)S(1)}, bf16[8,48,768]{2,1,0:T(8,128)(2,1)S(1)}, u32[]{:S(2)}, u32[]{:S(2)}) collective-permute-start(bf16[8,48,768]{2,1,0:T(8,128)(2,1)S(1)} %constant_dynamic-update-slice_fusion.12), channel_id=1, source_target_pairs={{0,8},{8,0},{16,24},{24,16},{1,9},{9,1},{17,25},{25,17},{2,10},{10... | collective-permute-start | bytes 1769480 | tf_op jit(solution)/shard_map/ppermute | solution.py:576
  (58 other events, 383.4 us)
